TPU v7x, 128 devices: a whole 4x4x4 slice. The times are simulated.
128 devices in a mesh: hst: 16 (over z, x), head: 8 (over y, core).
Axes of the slice: x: 4, y: 4, z: 4, core: 2. Of those that a mesh axis runs over, the one named last changes fastest.
Arguments:
- fresh_states: bfloat16 [8192, 8192], P('hst'), may hold values from -60 to 60
- query_states: bfloat16 [128, 8192], P('hst'), may hold values from -60 to 60
- w_query: bfloat16 [8192, 8192], P('hst', 'head'), may hold values from -0.0625 to 0.0625
- w_key: bfloat16 [8192, 1024], P('hst', 'head'), may hold values from -0.0625 to 0.0625
- w_value: bfloat16 [8192, 1024], P('hst', 'head'), may hold values from -0.0625 to 0.0625
- w_output: bfloat16 [8192, 8192], P('head', 'hst'), may hold values from -0.0625 to 0.0625
- cache_keys: bfloat16 [256, 256, 1024], P('hst', None, 'head'), may hold values from -6 to 6
- cache_values: bfloat16 [256, 256, 1024], P('hst', None, 'head'), may hold values from -6 to 6
- cached_mask: int32 [256], P('hst'), may hold values 0 or 1
- fresh_ids: int32 [32], P('hst'), may hold values from 0 to 255
- anchor_id: int32 [1], replicated, may hold values from 0 to 255
- query_pos: int32 [128], P('hst'), may hold values from 65536 to 65791
Outputs:
- fresh_context: bfloat16 [8192, 8192], P('hst', 'head')
- query_output: bfloat16 [128, 8192], P('head', 'hst')
All inputs are finite; a program needn't handle non-finite values. No bound on the sum of `cached_mask` on one device may be relied on, other than what follows from the above.
Results may differ from a plain program's by a relative error of at most 0.039.
Values may be sent and summed in bfloat16 or wider, within the bound.
No kernel may reach another device: no remote copies, remote signals or barrier semaphores. Data moves between devices by JAX's collectives and lax.ppermute only.
A program may use at most 192 MiB of HBM per device.

v0:
```python
import math

import jax
import jax.numpy as jnp
from jax import lax
from jax.sharding import PartitionSpec as P

HD = 128
BLK = 256
FRESH_BLK = 2


ROPE_BASE = 500000.0


def from_root(value, axis, root):
    mine = lax.axis_index(axis) == root
    return lax.psum(jnp.where(mine, value, jnp.zeros_like(value)), axis)


def scaled_rates(width):
    half = width // 2
    base_rates = ROPE_BASE ** (-jnp.arange(half, dtype=jnp.float32) * (2.0 / width))
    wavelength = 2.0 * math.pi / base_rates
    smooth = jnp.clip((8192.0 / wavelength - 1.0) / 3.0, 0.0, 1.0)
    return (1.0 - smooth) * base_rates / 8.0 + smooth * base_rates


def rotary(vectors, places):
    half = vectors.shape[-1] // 2
    rates = scaled_rates(vectors.shape[-1])
    angles = places.astype(jnp.float32)[:, None] * rates[None, :]
    cosine = jnp.cos(angles)[:, None, :]
    sine = jnp.sin(angles)[:, None, :]
    leading = vectors[..., :half]
    trailing = vectors[..., half:]
    return jnp.concatenate(
        [leading * cosine - trailing * sine, trailing * cosine + leading * sine], axis=-1
    )


def body(
    fresh_states,
    query_states,
    w_query,
    w_key,
    w_value,
    w_output,
    cache_keys,
    cache_values,
    cached_mask,
    fresh_ids,
    anchor_id,
    query_pos,
):
    fresh_rows = fresh_states.shape[0]
    query_rows = query_states.shape[0]
    query_cols = w_query.shape[1]
    key_cols = w_key.shape[1]
    local_heads = query_cols // HD
    local_groups = key_cols // HD
    per_group = local_heads // local_groups
    inverse_root = 1.0 / math.sqrt(HD)
    tokens = jnp.concatenate([fresh_states, query_states], axis=0)
    pieces = (
        lax.all_gather(w_query, "hst", axis=0, tiled=True),
        lax.all_gather(w_key, "hst", axis=0, tiled=True),
        lax.all_gather(w_value, "hst", axis=0, tiled=True),
    )
    query_all, key_all, value_all = tuple(
        (jnp.dot(tokens, weights, preferred_element_type=jnp.float32) for weights in pieces)
    )
    fresh_places = (fresh_ids[:, None] * BLK + jnp.arange(BLK, dtype=jnp.int32)[None, :]).reshape(
        -1
    )
    fresh_query = rotary(
        query_all[:fresh_rows].reshape(fresh_rows, local_heads, HD), fresh_places
    ).astype(jnp.bfloat16)
    fresh_key = rotary(
        key_all[:fresh_rows].reshape(fresh_rows, local_groups, HD), fresh_places
    ).astype(jnp.bfloat16)
    fresh_value = value_all[:fresh_rows].astype(jnp.bfloat16).reshape(fresh_rows, local_groups, HD)
    own_queries = rotary(
        query_all[fresh_rows:].reshape(query_rows, local_heads, HD), query_pos
    ).astype(jnp.bfloat16)
    all_queries = lax.all_gather(own_queries, "hst", axis=0, tiled=True)
    held_blocks = cache_keys.shape[0]
    anchor = anchor_id[0]
    anchor_key = lax.dynamic_index_in_dim(cache_keys, anchor % held_blocks, 0, keepdims=False)
    anchor_value = lax.dynamic_index_in_dim(cache_values, anchor % held_blocks, 0, keepdims=False)
    anchor_key, anchor_value = (
        from_root(anchor_key, "hst", anchor // held_blocks),
        from_root(anchor_value, "hst", anchor // held_blocks),
    )
    anchor_key = anchor_key.reshape(BLK, local_groups, HD)
    anchor_value = anchor_value.reshape(BLK, local_groups, HD)
    block_query = fresh_query.reshape(FRESH_BLK, BLK, local_groups, per_group, HD)
    block_key = fresh_key.reshape(FRESH_BLK, BLK, local_groups, HD)
    block_value = fresh_value.reshape(FRESH_BLK, BLK, local_groups, HD)
    anchor_scores = jnp.einsum(
        "bqkgd,skd->bkgqs", block_query, anchor_key, preferred_element_type=jnp.float32
    )
    own_scores = jnp.einsum(
        "bqkgd,bskd->bkgqs", block_query, block_key, preferred_element_type=jnp.float32
    )
    scores = jnp.concatenate([anchor_scores, own_scores], axis=-1) * inverse_root
    causal = jnp.arange(BLK)[None, :] <= jnp.arange(BLK)[:, None]
    allowed = jnp.concatenate([jnp.ones((BLK, BLK), bool), causal], axis=1)
    scores = jnp.where(allowed, scores, -jnp.inf)
    highest = jnp.max(scores, axis=-1, keepdims=True)
    raised = jnp.exp(scores - highest)
    probs = (raised / jnp.sum(raised, axis=-1, keepdims=True)).astype(jnp.bfloat16)
    both_values = jnp.concatenate(
        [jnp.broadcast_to(anchor_value[None], (FRESH_BLK, BLK, local_groups, HD)), block_value],
        axis=1,
    )
    mixed = jnp.einsum("bkgqs,bskd->bqkgd", probs, both_values, preferred_element_type=jnp.float32)
    fresh_context = mixed.astype(jnp.bfloat16).reshape(fresh_rows, query_cols)
    grouped = all_queries.reshape(all_queries.shape[0], local_groups, per_group, HD)
    context_keys = jnp.concatenate([cache_keys.reshape(-1, local_groups, HD), fresh_key], axis=0)
    context_values = jnp.concatenate(
        [cache_values.reshape(-1, local_groups, HD), fresh_value], axis=0
    )
    live = jnp.concatenate([jnp.repeat(cached_mask == 1, BLK), jnp.ones((fresh_rows,), bool)])
    query_scores = (
        jnp.einsum("qkgd,skd->kgqs", grouped, context_keys, preferred_element_type=jnp.float32)
        * inverse_root
    )
    query_scores = jnp.where(live, query_scores, -jnp.inf)
    peaks = jnp.max(query_scores, axis=-1)
    lifted = jnp.exp(query_scores - peaks[..., None])
    totals = jnp.sum(lifted, axis=-1)
    weighted = jnp.einsum(
        "kgqs,skd->kgqd",
        lifted.astype(jnp.bfloat16),
        context_values,
        preferred_element_type=jnp.float32,
    )
    every_peak, every_total, every_weighted = (
        lax.all_gather(peaks[None], "hst", axis=0, tiled=True),
        lax.all_gather(totals[None], "hst", axis=0, tiled=True),
        lax.all_gather(weighted[None], "hst", axis=0, tiled=True),
    )
    peaks = jnp.max(every_peak, axis=0)
    factors = jnp.exp(every_peak - peaks)
    totals = jnp.sum(every_total * factors, axis=0)
    weighted = jnp.sum(every_weighted * factors[..., None], axis=0)
    query_context = (
        (weighted / totals[..., None])
        .transpose(2, 0, 1, 3)
        .reshape(-1, query_cols)
        .astype(jnp.bfloat16)
    )
    query_output = lax.psum_scatter(
        jnp.dot(query_context, w_output, preferred_element_type=jnp.float32),
        "head",
        scatter_dimension=0,
        tiled=True,
    )
    return (fresh_context, query_output.astype(jnp.bfloat16))


def solution(mesh):
    return jax.shard_map(
        body,
        mesh=mesh,
        in_specs=(
            P("hst", None),
            P("hst", None),
            P("hst", "head"),
            P("hst", "head"),
            P("hst", "head"),
            P("head", "hst"),
            P("hst", None, "head"),
            P("hst", None, "head"),
            P("hst"),
            P("hst"),
            P(),
            P("hst"),
        ),
        out_specs=(P("hst", "head"), P("head", "hst")),
        check_vma=False,
    )
```

profile of v0, /device:TPU:1, one launch (start us, length us, event | category | flops | bytes accessed | tf_op | source)
XLA Modules:
  0.0 422.4 jit_solution(14538675517773717079)
XLA Ops:
  7.2 0.7 all-gather.12.cloned.1.call-update
  8.0 0.7 all-gather.8.cloned.1.call-update
  8.7 0.7 all-gather.10.cloned.1.call-update
  10.1 1.5 select_bitcast_fusion
  11.6 1.5 select_bitcast_fusion.1
  13.2 7.6 %constant_dynamic-update-slice_fusion.1 = bf16[520,8192]{1,0:T(8,128)(2,1)} fusion(bf16[512,8192]{1,0:T(8,128)(2,1)} %param.12), kind=kLoop, calls=%fused_computation.77 | loop fusion | bytes 16777216
  21.1 0.7 constant_dynamic-update-slice_fusion
  21.8 35.8 %all-gather.12.cloned.1.call-done = bf16[8192,128]{1,0:T(8,128)(2,1)} async-done(((bf16[512,128]{1,0:T(8,128)(2,1)}), bf16[8192,128]{1,0:T(8,128)(2,1)}) %all-gather.12.cloned.1.call-update) | async-done | bytes 2097168 | tf_op jit(solution)/shard_map/all_gather | solution.py:67
  57.6 6.8 %fusion.29 = f32[512,1,128]{0,2,1:T(8,128)S(1)} fusion(bf16[8192,128]{1,0:T(8,128)(2,1)} %all-gather.12.cloned.1.call-done, bf16[520,8192]{1,0:T(8,128)(2,1)} %constant_dynamic-update-slice_fusion), kind=kOutput, calls=%fused_computation.32 | convolution fusion | flops 1073741824 | bytes 10747904 | tf_op jit(solution)/shard_map/dot_general | solution.py:71
  65.1 0.8 copy.43
  65.8 38.5 %all-gather.8.cloned.1.call-done = bf16[8192,128]{1,0:T(8,128)(2,1)} async-done(((bf16[512,128]{1,0:T(8,128)(2,1)}), bf16[8192,128]{1,0:T(8,128)(2,1)}) %all-gather.8.cloned.1.call-update) | async-done | bytes 2097168 | tf_op jit(solution)/shard_map/all_gather | solution.py:68
  104.3 6.4 %fusion.61 = bf16[520,128]{1,0:T(8,128)(2,1)S(1)} fusion(bf16[520,8192]{1,0:T(8,128)(2,1)} %constant_dynamic-update-slice_fusion, bf16[8192,128]{1,0:T(8,128)(2,1)} %all-gather.8.cloned.1.call-done), kind=kOutput, calls=%fused_computation.94 | convolution fusion | flops 1090519040 | bytes 10749952 | tf_op jit(solution)/shard_map/dot_general | solution.py:71
  111.4 0.7 slice_bitcast_fusion.1
  112.1 106.2 %all-gather.10.cloned.1.call-done = bf16[8192,1024]{1,0:T(8,128)(2,1)} async-done(((bf16[512,1024]{1,0:T(8,128)(2,1)}), bf16[8192,1024]{1,0:T(8,128)(2,1)}) %all-gather.10.cloned.1.call-update) | async-done | bytes 16777232 | tf_op jit(solution)/shard_map/all_gather | solution.py:66
  218.3 14.6 %fusion.62 = f32[520,1024]{1,0:T(8,128)S(1)} fusion(bf16[520,8192]{1,0:T(8,128)(2,1)} %constant_dynamic-update-slice_fusion, bf16[8192,1024]{1,0:T(8,128)(2,1)} %all-gather.10.cloned.1.call-done), kind=kOutput, calls=%fused_computation.95 | convolution fusion | flops 8724152320 | bytes 27426816 | tf_op jit(solution)/shard_map/dot_general | solution.py:71
  233.1 18.3 %all_gather.24 = bf16[128,8,128]{2,0,1:T(8,128)(2,1)S(1)} all-gather(bf16[8,8,128]{2,0,1:T(8,128)(2,1)S(1)} %pad_maximum_fusion.4), channel_id=1, replica_groups=mesh['hst'=16,'head'=8] {'hst'}, dimensions={0}, use_global_device_ids=true | all-gather | bytes 278528 | tf_op jit(solution)/shard_map/all_gather | solution.py:86
  251.4 2.6 bitcast_reduce_fusion
  254.1 6.5 %copy-done.3 = f32[4608,128,8]{1,0,2:T(8,128)} copy-done((f32[4608,128,8]{1,0,2:T(8,128)}, f32[4608,128,8]{1,0,2:T(8,128)S(1)}, u32[]{:S(2)}) %copy-start.3) | copy-done | bytes 18874392
  260.5 5.7 %fusion.4 = f32[8,128,128]{2,1,0:T(8,128)} fusion(f32[4608,128,8]{1,0,2:T(8,128)S(1)} %get-tuple-element.17, f32[8,128]{1,0:T(8,128)S(1)} %get-tuple-element.16, pred[4608]{0:T(1024)(128)(4,1)S(1)} %concatenate.90, bf16[512,1,128]{2,0,1:T(8,128)(2,1)S(1)} %copy-done.10, bf16[4096,1,128]{2,0,1:T(8,128)(2,1)S(1)} %bitcast.152), kind=kOutput, calls=%fused_computation.7 | convolution fusion | flops 1229193216 | bytes 20587008 | tf_op jit(solution)/shard_map/kgqs,skd->kgqd/dot_general | solution.py:133
  266.4 1.2 multiply_cosine_fusion.1
  267.6 34.7 %all-reduce.5.cloned.1.call-done = (bf16[256,128]{1,0:T(8,128)(2,1)}, bf16[256,128]{1,0:T(8,128)(2,1)}) async-done(((bf16[256,128]{1,0:T(8,128)(2,1)}, bf16[256,128]{1,0:T(8,128)(2,1)}), (bf16[256,128]{1,0:T(8,128)(2,1)}, bf16[256,128]{1,0:T(8,128)(2,1)})) %all-reduce.5.cloned.1.call-update) | async-done | bytes 131088 | tf_op jit(solution)/shard_map/psum | solution.py:18
  302.3 1.6 copy.33
  303.9 0.8 copy.52
  304.8 1.6 slice.70
  306.4 1.7 copy.34
  308.0 1.5 slice.43
  309.5 1.9 copy.53
  311.4 2.3 subtract_convert_fusion
  313.7 1.2 concatenate.81
  314.9 0.7 copy.38
  315.6 2.0 concatenate.80
  317.6 1.6 copy.37
  319.1 17.2 %all-gather.1 = f32[128,128]{1,0:T(8,128)S(1)} all-gather(f32[8,128]{1,0:T(8,128)S(1)} %get-tuple-element.16), channel_id=3, replica_groups=mesh['hst'=16,'head'=8] {'hst'}, dimensions={0}, use_global_device_ids=true | all-gather | bytes 69632 | tf_op jit(solution)/shard_map/all_gather | solution.py:140
  336.3 9.6 %fusion.1 = f32[8,128]{1,0:T(8,128)S(1)} fusion(f32[4608,128,8]{1,0,2:T(8,128)} %copy-done.3, f32[8,128]{1,0:T(8,128)S(1)} %get-tuple-element.16, pred[4608]{0:T(1024)(128)(4,1)S(1)} %concatenate.90), kind=kLoop, calls=%fused_computation.4 | loop fusion | flops 18873344 | bytes 18887168 | tf_op jit(solution)/shard_map/reduce_sum | solution.py:132
  345.9 20.0 %all-gather.2 = f32[128,128]{1,0:T(8,128)S(1)} all-gather(f32[8,128]{1,0:T(8,128)S(1)} %fusion.1), channel_id=4, replica_groups=mesh['hst'=16,'head'=8] {'hst'}, dimensions={0}, use_global_device_ids=true | all-gather | bytes 69632 | tf_op jit(solution)/shard_map/all_gather | solution.py:141
  365.9 0.9 fusion.40
  366.9 0.8 fusion.41
  367.7 0.9 fusion.15
  368.8 1.3 copy-done.2
  370.1 1.7 exponential_reduce_fusion
  371.8 5.0 %all-gather.14.cloned.1.call-done = f32[128,128,128]{2,1,0:T(8,128)} async-done(((f32[8,128,128]{2,1,0:T(8,128)}), f32[128,128,128]{2,1,0:T(8,128)}) %all-gather.14.cloned.1.call-update) | async-done | bytes 8388624 | tf_op jit(solution)/shard_map/all_gather | solution.py:142
  376.8 5.3 %multiply_reduce_fusion = f32[8,128,128]{2,1,0:T(8,128)S(1)} fusion(f32[16,1,8,128,128]{4,3,2,0,1:T(8,128)} %bitcast.141, f32[16,8,128]{2,1,0:T(8,128)S(1)} %get-tuple-element.8), kind=kLoop, calls=%fused_computation.18 | loop fusion | flops 4063232 | bytes 8978432 | tf_op jit(solution)/shard_map/reduce_sum | solution.py:147
  382.4 1.0 fusion.63
  383.5 5.9 %fusion.21 = bf16[2,256,1,8,128]{1,4,3,0,2:T(8,128)(2,1)S(1)} fusion(f32[2,8,256,256]{2,3,1,0:T(8,128)} %bitcast.137, f32[2,8,256,256]{2,3,1,0:T(8,128)} %bitcast.140, f32[2,8,256]{2,1,0:T(8,128)S(1)} %exponential_reduce_fusion, f32[2,8,256]{2,1,0:T(8,128)S(1)} %fusion.15, pred[256,512]{0,1:T(8,128)(4,1)S(1)} %concatenate.79, ...), kind=kOutput, calls=%fused_computation.24 | convolution fusion | flops 550502400 | bytes 9863168 | tf_op jit(solution)/shard_map/bkgqs,bskd->bqkgd/dot_general | solution.py:117
  389.4 0.8 copy.42
  390.2 1.2 copy.57
  391.4 22.7 %reduce-scatter.2.cloned.1.call-done = f32[16,512]{1,0:T(8,128)} async-done(((f32[128,512]{1,0:T(8,128)}), f32[16,512]{1,0:T(8,128)}) %reduce-scatter.2.cloned.1.call-update) | async-done | bytes 32784 | tf_op jit(solution)/shard_map/reduce_scatter | solution.py:154
  414.2 1.4 convert_element_type.72
  (64 shorter events, 2.8 us)
Async XLA Ops:
  7.2 375.3 %copy-start = (bf16[1024,512]{1,0:T(8,128)(2,1)S(1)}, bf16[1024,512]{1,0:T(8,128)(2,1)}, u32[]{:S(2)}) copy-start(bf16[1024,512]{1,0:T(8,128)(2,1)} %param.17) | copy-start | bytes 3145732
  7.2 50.5 %all-gather.12.cloned.1.call-start = ((), (), s32[]{:S(2)}) async-start(), calls=%async_computation.3 | async-start | bytes 2228224 | tf_op jit(solution)/shard_map/all_gather | solution.py:67
  7.9 96.4 %all-gather.8.cloned.1.call-start = ((), (), s32[]{:S(2)}) async-start(), calls=%async_computation.1 | async-start | bytes 2228224 | tf_op jit(solution)/shard_map/all_gather | solution.py:68
  8.7 209.6 %all-gather.10.cloned.1.call-start = ((), (), s32[]{:S(2)}) async-start(), calls=%async_computation.2 | async-start | bytes 17825792 | tf_op jit(solution)/shard_map/all_gather | solution.py:66
  9.4 292.9 %all-reduce.5.cloned.1.call-start = ((), (), s32[]{:S(2)}) async-start(), calls=%async_computation.6 | async-start | bytes 262144 | tf_op jit(solution)/shard_map/psum | solution.py:18
  13.1 363.7 %all-gather.14.cloned.1.call-start = ((), (), s32[]{:S(2)}) async-start(), calls=%async_computation.5 | async-start | bytes 8912896 | tf_op jit(solution)/shard_map/all_gather | solution.py:142
  13.2 7.7 %copy-start.14 = (s32[2]{0:T(128)S(1)}, s32[2]{0:T(128)}, u32[]{:S(2)}) copy-start(s32[2]{0:T(128)} %param.21) | copy-start | bytes 28
  13.2 7.8 %copy-start.15 = (s32[16]{0:T(128)S(1)}, s32[16]{0:T(128)}, u32[]{:S(2)}) copy-start(s32[16]{0:T(128)} %param.20) | copy-start | bytes 196
  13.2 7.9 %copy-start.16 = (s32[8]{0:T(128)S(1)}, s32[8]{0:T(128)}, u32[]{:S(2)}) copy-start(s32[8]{0:T(128)} %param.23) | copy-start | bytes 100
  13.2 7.9 %copy-start.7 = (bf16[8,8192]{1,0:T(8,128)(2,1)S(1)}, bf16[8,8192]{1,0:T(8,128)(2,1)}, u32[]{:S(2)}) copy-start(bf16[8,8192]{1,0:T(8,128)(2,1)} %param.13) | copy-start | bytes 393220
  110.7 0.7 copy-start.5
  218.3 33.1 %copy-start.9 = (bf16[512,1,128]{2,0,1:T(8,128)(2,1)S(1)}, bf16[512,1,128]{2,0,1:T(8,128)(2,1)}, u32[]{:S(2)}) copy-start(bf16[512,1,128]{2,0,1:T(8,128)(2,1)} %copy.43) | copy-start | bytes 393220
  218.3 33.1 %copy-start.12 = (bf16[16,256,128]{2,1,0:T(8,128)(2,1)S(1)}, bf16[16,256,128]{2,1,0:T(8,128)(2,1)}, u32[]{:S(2)}) copy-start(bf16[16,256,128]{2,1,0:T(8,128)(2,1)} %param.18) | copy-start | bytes 3145732
  251.4 9.1 %copy-start.10 = (bf16[512,1,128]{2,0,1:T(8,128)(2,1)S(1)}, bf16[512,1,128]{2,0,1:T(8,128)(2,1)}, u32[]{:S(2)}) copy-start(bf16[512,1,128]{2,0,1:T(8,128)(2,1)} %slice_bitcast_fusion.1) | copy-start | bytes 393220
  251.4 9.1 %copy-start.13 = (bf16[16,256,128]{2,1,0:T(8,128)(2,1)S(1)}, bf16[16,256,128]{2,1,0:T(8,128)(2,1)}, u32[]{:S(2)}) copy-start(bf16[16,256,128]{2,1,0:T(8,128)(2,1)} %param.19) | copy-start | bytes 3145732
  254.0 6.5 %copy-start.3 = (f32[4608,128,8]{1,0,2:T(8,128)}, f32[4608,128,8]{1,0,2:T(8,128)S(1)}, u32[]{:S(2)}) copy-start(f32[4608,128,8]{1,0,2:T(8,128)S(1)} %get-tuple-element.17) | copy-start | bytes 56623108
  266.3 147.9 %reduce-scatter.2.cloned.1.call-start = ((), (), s32[]{:S(2)}) async-start(), calls=%async_computation.4 | async-start | bytes 294912 | tf_op jit(solution)/shard_map/reduce_scatter | solution.py:154
  336.3 29.6 %copy-start.4 = (bf16[512,1,64]{2,0,1:T(8,128)(2,1)S(1)}, bf16[512,1,64]{2,0,1:T(8,128)(2,1)}, u32[]{:S(2)}) copy-start(bf16[512,1,64]{2,0,1:T(8,128)(2,1)} %copy.52) | copy-start | bytes 196612
  336.3 30.5 %copy-start.11 = (bf16[256,128]{1,0:T(8,128)(2,1)S(1)}, bf16[256,128]{1,0:T(8,128)(2,1)}, u32[]{:S(2)}) copy-start(bf16[256,128]{1,0:T(8,128)(2,1)} %get-tuple-element.2) | copy-start | bytes 196612
  366.8 2.0 copy-start.1
  367.7 2.4 copy-start.2
  370.0 13.5 %copy-start.6 = (bf16[256,128]{0,1:T(8,128)(2,1)S(1)}, bf16[256,128]{0,1:T(8,128)(2,1)}, u32[]{:S(2)}) copy-start(bf16[256,128]{0,1:T(8,128)(2,1)} %copy.33) | copy-start | bytes 196612
  370.0 13.5 %copy-start.8 = (bf16[2,256,1,128]{1,3,0,2:T(8,128)(2,1)S(1)}, bf16[2,256,1,128]{1,3,0,2:T(8,128)(2,1)}, u32[]{:S(2)}) copy-start(bf16[2,256,1,128]{1,3,0,2:T(8,128)(2,1)} %copy.34) | copy-start | bytes 393220
Sparse Core Ops, SparseCore 0:
  10.2 47.4 all-gather.11
  59.8 44.5 all-gather.7
  106.5 111.7 all-gather.9
  221.4 80.8 all-reduce.4
  304.6 72.1 all-gather.13
  383.6 30.4 reduce-scatter.1
where the time goes:
time: 425 us; the launch traced here: 422 us
  waiting for transfers between devices  245 us (58%)
  blocking collectives  55.5 us (13%)
  matrix products  44.8 us (11%)
  local copies, waits for them, and re-layouts  35.1 us (8%)
  other arithmetic  26.5 us (6%)
  between operations  15.2 us (4%)
    all_gather x1, waiting for transfers between devices, body(): lax.all_gather(w_query, 'hst', axis=0, tiled=True)  106 us
    all_gather x1, waiting for transfers between devices, body(): lax.all_gather(w_value, 'hst', axis=0, tiled=True)  38.5 us
    all_gather x1, waiting for transfers between devices, body(): lax.all_gather(w_key, 'hst', axis=0, tiled=True)  35.8 us
    psum x1, waiting for transfers between devices, from_root(): return lax.psum(jnp.where(mine, value, jnp.zeros_like(value)), axis)  34.7 us
    dot_general x3, matrix products, body(): jnp.dot(tokens, weights, preferred_element_type=jnp.float32)  27.8 us
    reduce_scatter x1, waiting for transfers between devices, body(): lax.psum_scatter(jnp.dot(query_context, w_output, preferred_element_type=...  22.7 us
    all_gather x1, blocking collectives, body(): lax.all_gather(totals[None], 'hst', axis=0, tiled=True)  20 us
    all_gather x1, blocking collectives, body(): all_queries = lax.all_gather(own_queries, 'hst', axis=0, tiled=True)  18.3 us
  transfers between devices with their start and end apart: 6, of which 6 were waited for; matrix products, arithmetic and copies ran while one was open for 21% of the time, Pallas kernels for 0%

commit v1 on v0

v1 whole, which is shorter than its diff:
```python
import functools
import math

import jax
import jax.numpy as jnp
from jax import lax
from jax.experimental import pallas as pl
from jax.experimental.pallas import tpu as pltpu
from jax.sharding import PartitionSpec as P

HD = 128
BLK = 256
FRESH_BLK = 2
ROPE_BASE = 500000.0
N_HST = 16
N_HEAD = 8
SCALE = math.log2(math.e) / math.sqrt(HD)
BF16 = jnp.bfloat16
F32 = jnp.float32
VMEM_LIMIT = 48 * 1024 * 1024


def scaled_rates(width):
    half = width // 2
    base_rates = ROPE_BASE ** (-jnp.arange(half, dtype=F32) * (2.0 / width))
    wavelength = 2.0 * math.pi / base_rates
    smooth = jnp.clip((8192.0 / wavelength - 1.0) / 3.0, 0.0, 1.0)
    return (1.0 - smooth) * base_rates / 8.0 + smooth * base_rates


def rotary_tables(places):
    angles = places.astype(F32)[:, None] * scaled_rates(HD)[None, :]
    cosine, sine = jnp.cos(angles), jnp.sin(angles)
    return (
        jnp.concatenate([cosine, cosine], axis=1),
        jnp.concatenate([-sine, sine], axis=1),
    )


def rotate(vectors, cosine, sine):
    rows, cols = vectors.shape
    split = vectors.reshape(rows, cols // HD, HD)
    swapped = jnp.concatenate([split[..., HD // 2 :], split[..., : HD // 2]], axis=-1)
    return (split * cosine[:, None, :] + swapped * sine[:, None, :]).reshape(rows, cols)


def dot_t(a, b):
    return lax.dot_general(a, b, (((1,), (1,)), ((), ())), preferred_element_type=F32)


def fresh_kernel(q_ref, cos_ref, sin_ref, k_ref, v_ref, ak_ref, av_ref, out_ref):
    q = q_ref[...]
    q = (q * cos_ref[...] + pltpu.roll(q, HD // 2, 1) * sin_ref[...]).astype(BF16)
    row = lax.broadcasted_iota(jnp.int32, (BLK, BLK), 0)
    col = lax.broadcasted_iota(jnp.int32, (BLK, BLK), 1)
    causal = col <= row
    for b in range(FRESH_BLK):
        rows = slice(b * BLK, (b + 1) * BLK)
        qb = q[rows]
        s0 = dot_t(qb, ak_ref[...]) * SCALE
        s1 = jnp.where(causal, dot_t(qb, k_ref[rows, :]) * SCALE, -jnp.inf)
        top = jnp.max(jnp.maximum(s0, s1), axis=1, keepdims=True)
        e0 = jnp.exp2(s0 - top)
        e1 = jnp.exp2(s1 - top)
        total = jnp.sum(e0 + e1, axis=1, keepdims=True)
        mixed = jnp.dot(e0.astype(BF16), av_ref[...], preferred_element_type=F32)
        mixed += jnp.dot(e1.astype(BF16), v_ref[rows, :], preferred_element_type=F32)
        out_ref[rows, :] = (mixed / total).astype(BF16)


def fresh_attention(q, cosine, sine, key, value, anchor_key, anchor_value):
    rows, cols = q.shape
    whole = lambda a: pl.BlockSpec(a.shape, lambda i: (0, 0))
    return pl.pallas_call(
        fresh_kernel,
        grid=(cols // HD,),
        in_specs=[pl.BlockSpec((rows, HD), lambda i: (0, i))]
        + [whole(a) for a in (cosine, sine, key, value, anchor_key, anchor_value)],
        out_specs=pl.BlockSpec((rows, HD), lambda i: (0, i)),
        out_shape=jax.ShapeDtypeStruct((rows, cols), BF16),
        compiler_params=pltpu.CompilerParams(vmem_limit_bytes=VMEM_LIMIT),
        cost_estimate=pl.CostEstimate(
            flops=rows * (cols // HD) * 2 * BLK * HD * 4,
            bytes_accessed=rows * cols * 6,
            transcendentals=rows * (cols // HD) * 2 * BLK,
        ),
        name="fresh_attention",
    )(q, cosine, sine, key, value, anchor_key, anchor_value)


CHUNK = 512
STEP_HEADS = 2


def context_kernel(q_ref, ck_ref, cv_ref, fk_ref, fv_ref, bias_ref, out_ref, stat_ref, s_ref):
    step = pl.program_id(0)
    rows = q_ref.shape[0]
    q = jnp.concatenate([q_ref[:, g * HD : (g + 1) * HD] for g in range(STEP_HEADS)], axis=0)
    cached = ck_ref.shape[0]
    parts = [(ck_ref, cv_ref, i, i) for i in range(0, cached, CHUNK)]
    parts += [(fk_ref, fv_ref, i, cached + i) for i in range(0, fk_ref.shape[0], CHUNK)]
    top = None
    for keys, _, at, place in parts:
        s = dot_t(q, keys[at : at + CHUNK, :]) * SCALE
        if keys is ck_ref:
            s = s + bias_ref[:, place : place + CHUNK]
        s_ref[:, place : place + CHUNK] = s
        for j in range(0, CHUNK, HD):
            top = s[:, j : j + HD] if top is None else jnp.maximum(top, s[:, j : j + HD])
    peak = jnp.max(top, axis=1, keepdims=True)
    total = jnp.zeros((q.shape[0], HD), F32)
    acc = jnp.zeros((q.shape[0], HD), F32)
    for _, values, at, place in parts:
        e = jnp.exp2(s_ref[:, place : place + CHUNK] - peak)
        for j in range(0, CHUNK, HD):
            total += e[:, j : j + HD]
        acc += jnp.dot(e.astype(BF16), values[at : at + CHUNK, :], preferred_element_type=F32)
    total = jnp.sum(total, axis=1, keepdims=True)

    @pl.when(step == 0)
    def _():
        stat_ref[...] = jnp.zeros_like(stat_ref)

    lane = lax.broadcasted_iota(jnp.int32, (rows, HD), 1)
    stats = stat_ref[...]
    for g in range(STEP_HEADS):
        block = slice(g * rows, (g + 1) * rows)
        out_ref[:, g * HD : (g + 1) * HD] = acc[block]
        head = step * STEP_HEADS + g
        stats = jnp.where(lane == head, peak[block], stats)
        stats = jnp.where(lane == head + N_HEAD, total[block], stats)
    stat_ref[...] = stats


def context_attention(q, cache_key, cache_value, key, value, bias):
    rows, cols = q.shape
    heads = cols // HD
    wide = STEP_HEADS * HD
    keys = cache_key.shape[0] + key.shape[0]
    whole = lambda a: pl.BlockSpec(a.shape, lambda i: (0, 0))
    return pl.pallas_call(
        context_kernel,
        grid=(heads // STEP_HEADS,),
        in_specs=[pl.BlockSpec((rows, wide), lambda i: (0, i))]
        + [whole(a) for a in (cache_key, cache_value, key, value, bias)],
        out_specs=[
            pl.BlockSpec((rows, wide), lambda i: (0, i)),
            pl.BlockSpec((rows, HD), lambda i: (0, 0)),
        ],
        out_shape=[
            jax.ShapeDtypeStruct((rows, cols), F32),
            jax.ShapeDtypeStruct((rows, HD), F32),
        ],
        scratch_shapes=[pltpu.VMEM((STEP_HEADS * rows, keys), F32)],
        compiler_params=pltpu.CompilerParams(vmem_limit_bytes=VMEM_LIMIT),
        cost_estimate=pl.CostEstimate(
            flops=rows * heads * keys * HD * 4,
            bytes_accessed=keys * HD * 4 + rows * cols * 6,
            transcendentals=rows * heads * keys,
        ),
        name="context_attention",
    )(q, cache_key, cache_value, key, value, bias)


def exchange(value, axis):
    return lax.all_to_all(value, axis, 0, 0, tiled=True)


def spread(value, axis, count):
    return exchange(jnp.broadcast_to(value[None], (count,) + value.shape), axis)


def body(
    fresh_states,
    query_states,
    w_query,
    w_key,
    w_value,
    w_output,
    cache_keys,
    cache_values,
    cached_mask,
    fresh_ids,
    anchor_id,
    query_pos,
):
    fresh_rows = fresh_states.shape[0]
    query_rows, width = query_states.shape
    depth, query_cols = w_query.shape
    held_blocks = cache_keys.shape[0]

    w_both = lax.all_gather(
        jnp.concatenate([w_key, w_value], axis=1), "hst", axis=0, tiled=True
    )
    w_query_all = lax.all_gather(w_query, "hst", axis=0, tiled=True)

    anchor = anchor_id[0]
    mine = lax.axis_index("hst") == anchor // held_blocks
    slot = anchor % held_blocks
    anchor_parts = [
        jnp.where(mine, lax.dynamic_index_in_dim(a, slot, 0, keepdims=False), 0).reshape(
            N_HST, -1, depth
        )
        for a in (cache_keys, cache_values)
    ]
    states = query_states.reshape(query_rows, N_HST, depth).transpose(1, 0, 2)
    got = exchange(jnp.concatenate([states] + anchor_parts, axis=1), "hst")
    own_anchor = jnp.sum(got[:, query_rows:].astype(F32), axis=0).astype(BF16)
    states = got[:, :query_rows].reshape(N_HST * query_rows, depth)

    partial = jnp.dot(states, w_query, preferred_element_type=F32).astype(BF16)
    partial = exchange(partial.reshape(N_HST, query_rows, query_cols), "hst")
    query_cos, query_sin = rotary_tables(query_pos)
    own_queries = rotate(jnp.sum(partial.astype(F32), axis=0), query_cos, query_sin).astype(BF16)
    packed = jnp.concatenate([own_queries, own_anchor.reshape(-1, query_cols)], axis=0)
    packed = spread(packed, "hst", N_HST)
    all_queries = packed[:, :query_rows].reshape(N_HST * query_rows, query_cols)
    anchors = packed[:, query_rows:].reshape(N_HST, 2, BLK // N_HST, HD)
    anchor_key = anchors[:, 0].reshape(BLK, HD)
    anchor_value = anchors[:, 1].reshape(BLK, HD)

    places = (fresh_ids[:, None] * BLK + jnp.arange(BLK, dtype=jnp.int32)[None, :]).reshape(-1)
    cosine, sine = rotary_tables(places)
    both = jnp.dot(fresh_states, w_both, preferred_element_type=F32)
    fresh_key = rotate(both[:, :HD], cosine, sine).astype(BF16)
    fresh_value = both[:, HD:].astype(BF16)

    live = jnp.repeat(cached_mask == 1, BLK)
    bias = jnp.where(live, 0.0, -jnp.inf).astype(F32)[None, :]
    weighted, stats = context_attention(
        all_queries,
        cache_keys.reshape(-1, HD),
        cache_values.reshape(-1, HD),
        fresh_key,
        fresh_value,
        bias,
    )
    sums = exchange(
        jnp.concatenate([weighted, stats], axis=1).reshape(N_HST, query_rows, -1), "hst"
    )
    weighted = sums[..., :query_cols].reshape(N_HST, query_rows, N_HEAD, HD)
    peaks = sums[..., query_cols : query_cols + N_HEAD]
    totals = sums[..., query_cols + N_HEAD : query_cols + 2 * N_HEAD]
    factors = jnp.exp2(peaks - jnp.max(peaks, axis=0))
    total = jnp.sum(totals * factors, axis=0)
    context = jnp.sum(weighted * factors[..., None], axis=0) / total[..., None]
    context = spread(context.reshape(query_rows, query_cols).astype(BF16), "hst", N_HST)
    product = jnp.dot(
        context.reshape(N_HST * query_rows, query_cols), w_output, preferred_element_type=F32
    )
    product = exchange(product.reshape(N_HEAD, -1, product.shape[1]), "head")
    query_output = jnp.sum(product, axis=0).astype(BF16)

    query = jnp.dot(fresh_states, w_query_all, preferred_element_type=F32)
    fresh_context = fresh_attention(
        query, cosine, sine, fresh_key, fresh_value, anchor_key, anchor_value
    )
    return fresh_context, query_output


def solution(mesh):
    return jax.shard_map(
        body,
        mesh=mesh,
        in_specs=(
            P("hst", None),
            P("hst", None),
            P("hst", "head"),
            P("hst", "head"),
            P("hst", "head"),
            P("head", "hst"),
            P("hst", None, "head"),
            P("hst", None, "head"),
            P("hst"),
            P("hst"),
            P(),
            P("hst"),
        ),
        out_specs=(P("hst", "head"), P("head", "hst")),
        check_vma=False,
    )
```

time: 425 us -> 221 us (0.52)
  waiting for transfers between devices: 245 us -> 95.2 us
  local copies, waits for them, and re-layouts: 35.1 us -> 2.55 us
  starting transfers between devices: 0.24 us -> 23.2 us
  blocking collectives: 55.5 us -> 33.6 us
  matrix products: 44.8 us -> 24.6 us
  Pallas kernels: 0 us -> 16.6 us
  other arithmetic: 26.5 us -> 9.95 us
    all_gather x4 -> x2, waiting for transfers between devices: 186 us -> 62.5 us  [the longest x1 53.8 us: body(): w_query_all = lax.all_gather(w_query, 'hst', axis=0, tiled=True)]
    all_gather x3 -> x0, blocking collectives: 55.5 us -> none  [the longest x1 20 us: body(): lax.all_gather(totals[None], 'hst', axis=0, tiled=True)]
    psum x1 -> x0, waiting for transfers between devices: 34.7 us -> none  [from_root(): return lax.psum(jnp.where(mine, value, jnp.zeros_like(value)), axis)]
    all_to_all x0 -> x2, blocking collectives: none -> 33.6 us  [exchange(): return lax.all_to_all(value, axis, 0, 0, tiled=True)]
    all_to_all x0 -> x4, waiting for transfers between devices: none -> 32 us  [exchange(): return lax.all_to_all(value, axis, 0, 0, tiled=True)]
    all_to_all x0 -> x4, starting transfers between devices: none -> 23.2 us  [exchange(): return lax.all_to_all(value, axis, 0, 0, tiled=True)]
    reduce_scatter x1 -> x0, waiting for transfers between devices: 22.7 us -> none  [body(): lax.psum_scatter(jnp.dot(query_context, w_output, preferred_element_type=...]
    dot_general x9 -> x4, matrix products: 44.8 us -> 24.6 us  [the longest x1 14.3 us: body(): query = jnp.dot(fresh_states, w_query_all, preferred_element_type=F32)]
  transfers between devices with their start and end apart: 6 -> 6, of which waited for: 6 -> 6; matrix products, arithmetic and copies ran while one was open for 21% -> 10% of each run, Pallas kernels for 0% -> 4%
where the time goes in v1:
time: 221 us
  waiting for transfers between devices  95.2 us (43%)
  blocking collectives  33.6 us (15%)
  matrix products  24.6 us (11%)
  starting transfers between devices  23.2 us (10%)
  Pallas kernels  16.6 us (8%)
  between operations  14.9 us (7%)
  other arithmetic  9.95 us (5%)
  local copies, waits for them, and re-layouts  2.55 us (1%)
    all_gather x1, waiting for transfers between devices, body(): w_query_all = lax.all_gather(w_query, 'hst', axis=0, tiled=True)  53.8 us
    all_to_all x2, blocking collectives, exchange(): return lax.all_to_all(value, axis, 0, 0, tiled=True)  33.6 us
    all_to_all x4, waiting for transfers between devices, exchange(): return lax.all_to_all(value, axis, 0, 0, tiled=True)  32 us
    all_to_all x4, starting transfers between devices, exchange(): return lax.all_to_all(value, axis, 0, 0, tiled=True)  23.2 us
    dot_general x1, matrix products, body(): query = jnp.dot(fresh_states, w_query_all, preferred_element_type=F32)  14.3 us
    pallas_call x1, Pallas kernels, context_attention(): pl.pallas_call(context_kernel, grid=(heads // STEP_HEADS,), in_specs=[pl....  8.83 us
    all_gather x1, waiting for transfers between devices, body(): lax.all_gather(jnp.concatenate([w_key, w_value], axis=1), 'hst', axis=0,...  8.73 us
    pallas_call x1, Pallas kernels, fresh_attention(): pl.pallas_call(fresh_kernel, grid=(cols // HD,), in_specs=[pl.BlockSpec((...  7.79 us
  transfers between devices with their start and end apart: 6, of which 6 were waited for; matrix products, arithmetic and copies ran while one was open for 10% of the time, Pallas kernels for 4%

profile of v1, /device:TPU:1, one launch (start us, length us, event | category | flops | bytes accessed | tf_op | source)
XLA Modules:
  0.0 220.7 jit_solution(9372379452029863101)
XLA Ops:
  7.2 0.0 copy-start
  7.2 0.0 all-gather.5.cloned.1.call-start
  7.2 1.8 pad_maximum_fusion.2
  9.0 0.0 all-gather.5.cloned.1.call-update
  9.0 0.0 all-gather.3.cloned.1.call-start
  9.1 0.7 all-gather.3.cloned.1.call-update
  10.5 0.9 dynamic-slice_select_fusion
  11.4 1.7 pad_maximum_fusion.3
  13.1 8.4 %all-to-all-start = ((bf16[16,16,512]{2,1,0:T(8,128)(2,1)}), bf16[16,16,512]{2,1,0:T(8,128)(2,1)S(1)}, u32[]{:S(2)}, u32[]{:S(2)}) async-start(bf16[16,16,512]{2,1,0:T(8,128)(2,1)} %pad_maximum_fusion.3), calls=%async_computation | async-start | bytes 524288 | tf_op jit(solution)/shard_map/all_to_all | solution.py:166
  21.5 0.7 broadcast_multiply_fusion
  22.2 0.1 convert_bitcast_fusion
  22.3 0.7 convert_element_type.46
  23.0 0.1 multiply_cosine_fusion.1
  23.1 6.1 %all-to-all-done = bf16[16,16,512]{2,1,0:T(8,128)(2,1)S(1)} async-done(((bf16[16,16,512]{2,1,0:T(8,128)(2,1)}), bf16[16,16,512]{2,1,0:T(8,128)(2,1)S(1)}, u32[]{:S(2)}, u32[]{:S(2)}) %all-to-all-start) | async-done | bytes 262176 | tf_op jit(solution)/shard_map/all_to_all | solution.py:166
  29.2 2.2 %fusion = bf16[16,8,1024]{2,1,0:T(8,128)(2,1)} fusion(bf16[512,1024]{1,0:T(8,128)(2,1)} %param.14, bf16[16,16,512]{2,1,0:T(8,128)(2,1)S(1)} %all-to-all-done), kind=kOutput, calls=%fused_computation.2 | convolution fusion | flops 134348800 | bytes 1441792 | tf_op jit(solution)/shard_map/dot_general | solution.py:211
  31.4 3.5 %all-to-all-start.1 = ((bf16[16,8,1024]{2,1,0:T(8,128)(2,1)}), bf16[16,8,1024]{2,1,0:T(8,128)(2,1)S(1)}, u32[]{:S(2)}, u32[]{:S(2)}) async-start(bf16[16,8,1024]{2,1,0:T(8,128)(2,1)} %fusion), calls=%async_computation.1 | async-start | bytes 524288 | tf_op jit(solution)/shard_map/all_to_all | solution.py:166
  34.9 0.7 compare_select_fusion
  35.6 0.1 pad_maximum_fusion.5
  35.7 6.7 %all-to-all-done.1 = bf16[16,8,1024]{2,1,0:T(8,128)(2,1)S(1)} async-done(((bf16[16,8,1024]{2,1,0:T(8,128)(2,1)}), bf16[16,8,1024]{2,1,0:T(8,128)(2,1)S(1)}, u32[]{:S(2)}, u32[]{:S(2)}) %all-to-all-start.1) | async-done | bytes 262176 | tf_op jit(solution)/shard_map/all_to_all | solution.py:166
  42.5 0.1 fusion.14
  42.6 0.1 fusion.10
  42.7 0.9 broadcast_in_dim.18
  43.5 3.6 %all-to-all-start.2 = ((bf16[16,12,1024]{2,1,0:T(8,128)(2,1)}), bf16[16,12,1024]{2,1,0:T(8,128)(2,1)S(1)}, u32[]{:S(2)}, u32[]{:S(2)}) async-start(bf16[16,12,1024]{2,1,0:T(8,128)(2,1)} %broadcast_in_dim.18), calls=%async_computation.2 | async-start | bytes 1048576 | tf_op jit(solution)/shard_map/all_to_all | solution.py:166
  47.1 0.1 broadcast_bitcast_fusion
  47.2 1.8 fusion.6
  49.0 13.7 %all-to-all-done.2 = bf16[16,12,1024]{2,1,0:T(8,128)(2,1)S(1)} async-done(((bf16[16,12,1024]{2,1,0:T(8,128)(2,1)}), bf16[16,12,1024]{2,1,0:T(8,128)(2,1)S(1)}, u32[]{:S(2)}, u32[]{:S(2)}) %all-to-all-start.2) | async-done | bytes 393248 | tf_op jit(solution)/shard_map/all_to_all | solution.py:166
  62.8 0.0 copy-start.1
  62.8 8.7 %all-gather.5.cloned.1.call-done = bf16[8192,256]{1,0:T(8,128)(2,1)} async-done(((bf16[512,256]{1,0:T(8,128)(2,1)}), bf16[8192,256]{1,0:T(8,128)(2,1)}) %all-gather.5.cloned.1.call-update) | async-done | bytes 4194320 | tf_op jit(solution)/shard_map/all_gather | solution.py:192
  71.5 7.0 %convolution_bitcast_fusion = f32[512,256]{1,0:T(8,128)S(1)} fusion(bf16[512,8192]{1,0:T(8,128)(2,1)} %param.12, bf16[8192,256]{1,0:T(8,128)(2,1)} %all-gather.5.cloned.1.call-done), kind=kOutput, calls=%fused_computation | convolution fusion | flops 2147483648 | bytes 13107200 | tf_op jit(solution)/shard_map/dot_general | solution.py:224
  78.6 0.1 slice_bitcast_fusion.2
  78.8 0.3 fusion.5
  79.1 8.8 %context_attention.1 = (f32[128,1024]{1,0:T(8,128)S(1)}, f32[128,128]{1,0:T(8,128)S(1)}) custom-call(bf16[128,1024]{1,0:T(8,128)(2,1)S(1)} %slice_bitcast_fusion.q_ref, bf16[4096,128]{1,0:T(8,128)(2,1)S(1)} %bitcast.71, bf16[4096,128]{1,0:T(8,128)(2,1)S(1)} %bitcast.70, bf16[512,128]{1,0:T(8,128)(2,1)S(1)} %get-tuple-element.8.k_ref.fk_ref, ...), custom_call_target="tpu_custom_call" | custom-call | flops 2415919104 | bytes 3145728 | tf_op jit(solution)/shard_map/context_attention/pallas_call | solution.py:141
  88.0 23.4 %all_to_all.30 = f32[16,8,1152]{2,1,0:T(8,128)S(1)} all-to-all(f32[16,8,1152]{2,1,0:T(8,128)S(1)} %maximum_bitcast_fusion), channel_id=1, replica_groups=mesh['hst'=16,'head'=8] {'hst'}, dimensions={0} | all-to-all | bytes 1179648 | tf_op jit(solution)/shard_map/all_to_all | solution.py:166
  111.4 0.1 fusion.7
  111.5 0.1 copy.21
  111.6 0.1 copy.22
  111.6 0.2 fusion.3
  111.9 0.1 fusion.11
  112.0 10.2 %all_to_all.31 = bf16[16,8,1024]{2,1,0:T(8,128)(2,1)S(1)} all-to-all(bf16[16,8,1024]{2,1,0:T(8,128)(2,1)S(1)} %broadcast_in_dim.24), channel_id=1, replica_groups=mesh['hst'=16,'head'=8] {'hst'}, dimensions={0} | all-to-all | bytes 524288 | tf_op jit(solution)/shard_map/all_to_all | solution.py:166
  122.1 1.0 fusion.1
  123.2 7.6 %all-to-all-start.5 = ((f32[8,16,512]{2,1,0:T(8,128)}), f32[8,16,512]{2,1,0:T(8,128)S(1)}, u32[]{:S(2)}, u32[]{:S(2)}) async-start(f32[8,16,512]{2,1,0:T(8,128)} %fusion.1), calls=%async_computation.5 | async-start | bytes 524288 | tf_op jit(solution)/shard_map/all_to_all | solution.py:166
  130.8 1.0 slice.69
  131.8 0.1 reshape.140
  131.9 5.5 %all-to-all-done.5 = f32[8,16,512]{2,1,0:T(8,128)S(1)} async-done(((f32[8,16,512]{2,1,0:T(8,128)}), f32[8,16,512]{2,1,0:T(8,128)S(1)}, u32[]{:S(2)}, u32[]{:S(2)}) %all-to-all-start.5) | async-done | bytes 262176 | tf_op jit(solution)/shard_map/all_to_all | solution.py:166
  137.3 0.6 reduce_sum.52
  138.0 53.8 %all-gather.3.cloned.1.call-done = bf16[8192,1024]{1,0:T(8,128)(2,1)} async-done(((bf16[512,1024]{1,0:T(8,128)(2,1)}), bf16[8192,1024]{1,0:T(8,128)(2,1)}) %all-gather.3.cloned.1.call-update) | async-done | bytes 16777232 | tf_op jit(solution)/shard_map/all_gather | solution.py:195
  191.8 14.3 %fusion.15.q_ref = f32[512,1024]{1,0:T(8,128)S(1)} fusion(bf16[512,8192]{1,0:T(8,128)(2,1)} %param.12, bf16[8192,1024]{1,0:T(8,128)(2,1)} %all-gather.3.cloned.1.call-done), kind=kOutput, calls=%fused_computation.52 | convolution fusion | flops 8589934592 | bytes 27262976 | tf_op jit(solution)/shard_map/dot_general | solution.py:254
  206.1 7.8 %fresh_attention.1 = bf16[512,1024]{1,0:T(8,128)(2,1)} custom-call(f32[512,1024]{1,0:T(8,128)S(1)} %fusion.15.q_ref, f32[512,128]{1,0:T(8,128)S(1)} %get-tuple-element.10.cos_ref, f32[512,128]{1,0:T(8,128)S(1)} %get-tuple-element.9.sin_ref, bf16[512,128]{1,0:T(8,128)(2,1)S(1)} %get-tuple-element.8.k_ref.fk_ref, bf16[512,128]{1,0:T(8,128)(2,1)S(1)} %slice.93.v_ref.fv_ref, ...), custom_call_target="tpu_custom_call" | custom-call | flops 1073741824 | bytes 3145728 | tf_op jit(solution)/shard_map/fresh_attention/pallas_call | solution.py:74
  (26 shorter events, 0.4 us)
Async XLA Ops:
  7.2 115.0 %copy-start = (bf16[1024,512]{1,0:T(8,128)(2,1)S(1)}, bf16[1024,512]{1,0:T(8,128)(2,1)}, u32[]{:S(2)}) copy-start(bf16[1024,512]{1,0:T(8,128)(2,1)} %param.17) | copy-start | bytes 3145732
  7.2 64.3 %all-gather.5.cloned.1.call-start = ((), (), s32[]{:S(2)}) async-start(), calls=%async_computation.7 | async-start | bytes 4456448 | tf_op jit(solution)/shard_map/all_gather | solution.py:192
  9.0 182.8 %all-gather.3.cloned.1.call-start = ((), (), s32[]{:S(2)}) async-start(), calls=%async_computation.6 | async-start | bytes 17825792 | tf_op jit(solution)/shard_map/all_gather | solution.py:195
  13.1 16.1 %all-to-all-start = ((bf16[16,16,512]{2,1,0:T(8,128)(2,1)}), bf16[16,16,512]{2,1,0:T(8,128)(2,1)S(1)}, u32[]{:S(2)}, u32[]{:S(2)}) async-start(bf16[16,16,512]{2,1,0:T(8,128)(2,1)} %pad_maximum_fusion.3), calls=%async_computation | async-start | bytes 524288 | tf_op jit(solution)/shard_map/all_to_all | solution.py:166
  31.4 11.0 %all-to-all-start.1 = ((bf16[16,8,1024]{2,1,0:T(8,128)(2,1)}), bf16[16,8,1024]{2,1,0:T(8,128)(2,1)S(1)}, u32[]{:S(2)}, u32[]{:S(2)}) async-start(bf16[16,8,1024]{2,1,0:T(8,128)(2,1)} %fusion), calls=%async_computation.1 | async-start | bytes 524288 | tf_op jit(solution)/shard_map/all_to_all | solution.py:166
  43.5 19.2 %all-to-all-start.2 = ((bf16[16,12,1024]{2,1,0:T(8,128)(2,1)}), bf16[16,12,1024]{2,1,0:T(8,128)(2,1)S(1)}, u32[]{:S(2)}, u32[]{:S(2)}) async-start(bf16[16,12,1024]{2,1,0:T(8,128)(2,1)} %broadcast_in_dim.18), calls=%async_computation.2 | async-start | bytes 1048576 | tf_op jit(solution)/shard_map/all_to_all | solution.py:166
  62.8 8.8 %copy-start.3 = (bf16[16,12,1024]{2,1,0:T(8,128)(2,1)}, bf16[16,12,1024]{2,1,0:T(8,128)(2,1)S(1)}, u32[]{:S(2)}) copy-start(bf16[16,12,1024]{2,1,0:T(8,128)(2,1)S(1)} %all-to-all-done.2) | copy-start | bytes 1179652
  62.8 16.3 %copy-start.1 = (bf16[16,256,128]{2,1,0:T(8,128)(2,1)S(1)}, bf16[16,256,128]{2,1,0:T(8,128)(2,1)}, u32[]{:S(2)}) copy-start(bf16[16,256,128]{2,1,0:T(8,128)(2,1)} %param.19) | copy-start | bytes 3145732
  71.5 7.2 %copy-start.4 = (f32[512,64]{1,0:T(8,128)S(1)}, f32[512,64]{1,0:T(8,128)}, u32[]{:S(2)}) copy-start(f32[512,64]{1,0:T(8,128)} %get-tuple-element.18) | copy-start | bytes 393220
  71.5 7.2 %copy-start.5 = (f32[512,64]{1,0:T(8,128)S(1)}, f32[512,64]{1,0:T(8,128)}, u32[]{:S(2)}) copy-start(f32[512,64]{1,0:T(8,128)} %get-tuple-element.19) | copy-start | bytes 393220
  71.5 7.5 %copy-start.2 = (bf16[16,256,128]{2,1,0:T(8,128)(2,1)S(1)}, bf16[16,256,128]{2,1,0:T(8,128)(2,1)}, u32[]{:S(2)}) copy-start(bf16[16,256,128]{2,1,0:T(8,128)(2,1)} %param.18) | copy-start | bytes 3145732
  123.2 14.2 %all-to-all-start.5 = ((f32[8,16,512]{2,1,0:T(8,128)}), f32[8,16,512]{2,1,0:T(8,128)S(1)}, u32[]{:S(2)}, u32[]{:S(2)}) async-start(f32[8,16,512]{2,1,0:T(8,128)} %fusion.1), calls=%async_computation.5 | async-start | bytes 524288 | tf_op jit(solution)/shard_map/all_to_all | solution.py:166
Sparse Core Ops, SparseCore 0:
  10.2 61.3 all-gather.4
  73.7 118.0 all-gather.2

commit v2 on v1

v2 whole, which is shorter than its diff:
```python
import functools
import math

import jax
import jax.numpy as jnp
from jax import lax
from jax.experimental import pallas as pl
from jax.experimental.pallas import tpu as pltpu
from jax.sharding import Mesh
from jax.sharding import PartitionSpec as P

HD = 128
BLK = 256
FRESH_BLK = 2
ROPE_BASE = 500000.0
N_HST = 16
N_HEAD = 8
RING = 4
STEP_HEADS = 2
HST = ("z", "x")
HEAD = ("y", "core")
SCALE = math.log2(math.e) / math.sqrt(HD)
BF16 = jnp.bfloat16
F32 = jnp.float32
VMEM_LIMIT = 48 * 1024 * 1024
DEAD = -1e30


def scaled_rates(width):
    half = width // 2
    base_rates = ROPE_BASE ** (-jnp.arange(half, dtype=F32) * (2.0 / width))
    wavelength = 2.0 * math.pi / base_rates
    smooth = jnp.clip((8192.0 / wavelength - 1.0) / 3.0, 0.0, 1.0)
    return (1.0 - smooth) * base_rates / 8.0 + smooth * base_rates


def rotary_tables(places):
    angles = places.astype(F32)[:, None] * scaled_rates(HD)[None, :]
    cosine, sine = jnp.cos(angles), jnp.sin(angles)
    return (
        jnp.concatenate([cosine, cosine], axis=1),
        jnp.concatenate([-sine, sine], axis=1),
    )


def rotate(vectors, cosine, sine):
    rows, cols = vectors.shape
    split = vectors.reshape(rows, cols // HD, HD)
    swapped = jnp.concatenate([split[..., HD // 2 :], split[..., : HD // 2]], axis=-1)
    return (split * cosine[:, None, :] + swapped * sine[:, None, :]).reshape(rows, cols)


def dot_t(a, b):
    return lax.dot_general(a, b, (((1,), (1,)), ((), ())), preferred_element_type=F32)


def fresh_kernel(count, *refs):
    parts, refs = refs[:count], refs[count:]
    cos_ref, sin_ref, k_ref, v_ref, ak_ref, av_ref, out_ref = refs
    row = lax.broadcasted_iota(jnp.int32, (BLK, BLK), 0)
    col = lax.broadcasted_iota(jnp.int32, (BLK, BLK), 1)
    causal = col <= row
    for g in range(out_ref.shape[1] // HD):
        cols = slice(g * HD, (g + 1) * HD)
        q = parts[0][:, cols].astype(F32)
        for part in parts[1:]:
            q += part[:, cols].astype(F32)
        q = (q * cos_ref[...] + pltpu.roll(q, HD // 2, 1) * sin_ref[...]).astype(BF16)
        for b in range(FRESH_BLK):
            rows = slice(b * BLK, (b + 1) * BLK)
            qb = q[rows]
            s0 = dot_t(qb, ak_ref[...]) * SCALE
            s1 = jnp.where(causal, dot_t(qb, k_ref[rows, :]) * SCALE, -jnp.inf)
            top = jnp.max(jnp.maximum(s0, s1), axis=1, keepdims=True)
            e0 = jnp.exp2(s0 - top)
            e1 = jnp.exp2(s1 - top)
            total = jnp.sum(e0 + e1, axis=1, keepdims=True)
            mixed = jnp.dot(e0.astype(BF16), av_ref[...], preferred_element_type=F32)
            mixed += jnp.dot(e1.astype(BF16), v_ref[rows, :], preferred_element_type=F32)
            out_ref[rows, cols] = (mixed / total).astype(BF16)


def fresh_attention(parts, rest):
    rows, cols = parts[0].shape
    wide = STEP_HEADS * HD
    whole = lambda a: pl.BlockSpec(a.shape, lambda i: (0, 0))
    return pl.pallas_call(
        functools.partial(fresh_kernel, len(parts)),
        grid=(cols // wide,),
        in_specs=[pl.BlockSpec((rows, wide), lambda i: (0, i))] * len(parts)
        + [whole(a) for a in rest],
        out_specs=pl.BlockSpec((rows, wide), lambda i: (0, i)),
        out_shape=jax.ShapeDtypeStruct((rows, cols), BF16),
        compiler_params=pltpu.CompilerParams(vmem_limit_bytes=VMEM_LIMIT),
        cost_estimate=pl.CostEstimate(
            flops=rows * (cols // HD) * 2 * BLK * HD * 4,
            bytes_accessed=rows * cols * 4,
            transcendentals=rows * (cols // HD) * 2 * BLK,
        ),
        name="fresh_attention",
    )(*parts, *rest)


def shares_kernel(count, place_ref, states_ref, *refs):
    pieces, w_refs = refs[:count], refs[count : count + 5]
    out_ref, t_v, w_v, o_v, t_sem, s_sem, w_sem, o_sem = refs[count + 5 :]
    blocks, rows, depth = t_v.shape
    slab = pieces[0].shape[1]
    own_copy = pltpu.make_async_copy(
        states_ref.at[:, pl.ds(pl.multiple_of(place_ref[0] * depth, depth), depth)],
        t_v.at[0],
        s_sem,
    )
    own_copy.start()
    w_copies = []
    for i, ref in enumerate(w_refs):
        at = pl.multiple_of(place_ref[blocks + count + i], slab)
        copy = pltpu.make_async_copy(ref, w_v.at[pl.ds(at, ref.shape[0]), :], w_sem.at[i])
        copy.start()
        w_copies.append(copy)
    copies = []
    for b in range(blocks - 1):
        for i, piece in enumerate(pieces):
            copy = pltpu.make_async_copy(
                piece.at[pl.ds(b * rows, rows), :],
                t_v.at[b + 1, :, pl.ds(pl.multiple_of(place_ref[blocks + i], slab), slab)],
                t_sem.at[b, i],
            )
            copy.start()
            copies.append(copy)
    own_copy.wait()
    for copy in w_copies:
        copy.wait()
    out_copies = []
    for b in range(blocks):
        if b > 0:
            for copy in copies[(b - 1) * count : b * count]:
                copy.wait()
        for n in range(0, w_v.shape[1], COLS):
            o_v[b, :, n : n + COLS] = jnp.dot(
                t_v[b], w_v[:, n : n + COLS], preferred_element_type=F32
            ).astype(BF16)
        copy = pltpu.make_async_copy(o_v.at[b], out_ref.at[place_ref[b]], o_sem.at[b])
        copy.start()
        out_copies.append(copy)
    for copy in out_copies:
        copy.wait()


def share_products(places, states, pieces, weights):
    blocks = RING
    rows = states.shape[0]
    depth = blocks * weights[0].shape[0]
    cols = weights[0].shape[1]
    anywhere = pl.BlockSpec(memory_space=pl.ANY)
    return pl.pallas_call(
        functools.partial(shares_kernel, len(pieces)),
        grid_spec=pltpu.PrefetchScalarGridSpec(
            num_scalar_prefetch=1,
            grid=(1,),
            in_specs=[anywhere] * (1 + len(pieces) + len(weights)),
            out_specs=anywhere,
            scratch_shapes=[
                pltpu.VMEM((blocks, rows, depth), BF16),
                pltpu.VMEM((depth, cols), BF16),
                pltpu.VMEM((blocks, rows, cols), BF16),
                pltpu.SemaphoreType.DMA((blocks - 1, len(pieces))),
                pltpu.SemaphoreType.DMA,
                pltpu.SemaphoreType.DMA((len(weights),)),
                pltpu.SemaphoreType.DMA((blocks,)),
            ],
        ),
        out_shape=jax.ShapeDtypeStruct((blocks, rows, cols), BF16),
        compiler_params=pltpu.CompilerParams(vmem_limit_bytes=VMEM_LIMIT),
        cost_estimate=pl.CostEstimate(
            flops=blocks * rows * depth * cols * 2,
            bytes_accessed=(blocks * rows * (depth + cols) + depth * cols) * 2,
            transcendentals=0,
        ),
        name="share_products",
    )(places, states, *pieces, *weights)


def key_value_kernel(states_ref, w_ref, cos_ref, sin_ref, k_ref, v_ref, acc_ref):
    step = pl.program_id(0)

    @pl.when(step == 0)
    def _():
        acc_ref[...] = jnp.zeros_like(acc_ref)

    acc_ref[...] += jnp.dot(states_ref[...], w_ref[...], preferred_element_type=F32)

    @pl.when(step == pl.num_programs(0) - 1)
    def _():
        k = acc_ref[:, :HD]
        k = k * cos_ref[...] + pltpu.roll(k, HD // 2, 1) * sin_ref[...]
        k_ref[...] = k.astype(BF16)
        v_ref[...] = acc_ref[:, HD:].astype(BF16)


def key_value(states, weights, cosine, sine):
    rows, depth = states.shape
    step = 1024
    whole = lambda a: pl.BlockSpec(a.shape, lambda i: (0, 0))
    out = jax.ShapeDtypeStruct((rows, HD), BF16)
    return pl.pallas_call(
        key_value_kernel,
        grid=(depth // step,),
        in_specs=[
            pl.BlockSpec((rows, step), lambda i: (0, i)),
            pl.BlockSpec((step, 2 * HD), lambda i: (i, 0)),
            whole(cosine),
            whole(sine),
        ],
        out_specs=[whole(out), whole(out)],
        out_shape=[out, out],
        scratch_shapes=[pltpu.VMEM((rows, 2 * HD), F32)],
        compiler_params=pltpu.CompilerParams(vmem_limit_bytes=VMEM_LIMIT),
        cost_estimate=pl.CostEstimate(
            flops=rows * depth * 4 * HD,
            bytes_accessed=(rows + 2 * HD) * depth * 2,
            transcendentals=0,
        ),
        name="key_value",
    )(states, weights, cosine, sine)


CHUNK = 512
COLS = 512


def pieces_of(value):
    high = value.astype(BF16).astype(F32)
    middle = (value - high).astype(BF16).astype(F32)
    return high, middle, value - high - middle


def cached_kernel(q_ref, k_ref, v_ref, bias_ref, out_ref, stat_ref, s_ref):
    step = pl.program_id(0)
    rows = q_ref.shape[0]
    q = jnp.concatenate([q_ref[:, g * HD : (g + 1) * HD] for g in range(STEP_HEADS)], axis=0)
    places = range(0, k_ref.shape[0], CHUNK)
    top = None
    for at in places:
        s = dot_t(q, k_ref[at : at + CHUNK, :]) * SCALE + bias_ref[:, at : at + CHUNK]
        s_ref[:, at : at + CHUNK] = s
        for j in range(0, CHUNK, HD):
            top = s[:, j : j + HD] if top is None else jnp.maximum(top, s[:, j : j + HD])
    peak = jnp.max(top, axis=1, keepdims=True)
    total = jnp.zeros((q.shape[0], HD), F32)
    acc = jnp.zeros((q.shape[0], HD), F32)
    for at in places:
        e = jnp.exp2(s_ref[:, at : at + CHUNK] - peak)
        for j in range(0, CHUNK, HD):
            total += e[:, j : j + HD]
        acc += jnp.dot(e.astype(BF16), v_ref[at : at + CHUNK, :], preferred_element_type=F32)
    total = jnp.sum(total, axis=1, keepdims=True)

    @pl.when(step == 0)
    def _():
        stat_ref[...] = jnp.zeros_like(stat_ref)

    lane = lax.broadcasted_iota(jnp.int32, (rows, HD), 1)
    stats = stat_ref[...]
    for g in range(STEP_HEADS):
        block = slice(g * rows, (g + 1) * rows)
        for n, number in enumerate((peak, total)):
            place = step * STEP_HEADS + g + n * N_HEAD
            stats = jnp.where(lane == place, number[block], stats)
        out_ref[:, g * HD : (g + 1) * HD] = acc[block]
    stat_ref[...] = stats


def cached_attention(q, key, value, bias):
    rows, cols = q.shape
    wide = STEP_HEADS * HD
    keys = key.shape[0]
    whole = lambda a: pl.BlockSpec(a.shape, lambda i: (0, 0))
    stats = jax.ShapeDtypeStruct((rows, HD), F32)
    return pl.pallas_call(
        cached_kernel,
        grid=(cols // wide,),
        in_specs=[pl.BlockSpec((rows, wide), lambda i: (0, i))]
        + [whole(a) for a in (key, value, bias)],
        out_specs=[pl.BlockSpec((rows, wide), lambda i: (0, i)), whole(stats)],
        out_shape=[jax.ShapeDtypeStruct((rows, cols), F32), stats],
        scratch_shapes=[pltpu.VMEM((STEP_HEADS * rows, keys), F32)],
        compiler_params=pltpu.CompilerParams(vmem_limit_bytes=VMEM_LIMIT),
        cost_estimate=pl.CostEstimate(
            flops=rows * cols * keys * 4,
            bytes_accessed=keys * HD * 4 + rows * cols * 4,
            transcendentals=rows * (cols // HD) * keys,
        ),
        name="cached_attention",
    )(q, key, value, bias)


def context_kernel(q_ref, k_ref, v_ref, old_ref, stat_ref, out_ref):
    rows, cols = q_ref.shape
    heads = cols // HD
    lane = lax.broadcasted_iota(jnp.int32, (rows, HD), 1)
    old_stats = stat_ref[...]
    stats = jnp.zeros((rows, HD), F32)
    for first in range(0, heads, STEP_HEADS):
        group = range(first, first + STEP_HEADS)
        q = jnp.concatenate([q_ref[:, g * HD : (g + 1) * HD] for g in group], axis=0)
        old = jnp.concatenate([old_ref[:, g * HD : (g + 1) * HD] for g in group], axis=0)
        old_peak = jnp.concatenate([old_stats[:, g : g + 1] for g in group], axis=0)
        old_total = jnp.concatenate(
            [old_stats[:, N_HEAD + g : N_HEAD + g + 1] for g in group], axis=0
        )
        s = dot_t(q, k_ref[...]) * SCALE
        peak = jnp.maximum(jnp.max(s, axis=1, keepdims=True), old_peak)
        e = jnp.exp2(s - peak)
        factor = jnp.exp2(old_peak - peak)
        total = jnp.sum(e, axis=1, keepdims=True) + old_total * factor
        acc = jnp.dot(e.astype(BF16), v_ref[...], preferred_element_type=F32) + old * factor
        numbers = pieces_of(peak) + pieces_of(total)
        for i, g in enumerate(group):
            block = slice(i * rows, (i + 1) * rows)
            for n, number in enumerate(numbers):
                stats = jnp.where(lane == g + n * N_HEAD, number[block], stats)
            out_ref[:, g * HD : (g + 1) * HD] = acc[block].astype(BF16)
    out_ref[:, cols:] = stats.astype(BF16)


def context_attention(q, key, value, old, old_stats):
    rows, cols = q.shape
    keys = key.shape[0]
    return pl.pallas_call(
        context_kernel,
        out_shape=jax.ShapeDtypeStruct((rows, cols + HD), BF16),
        compiler_params=pltpu.CompilerParams(vmem_limit_bytes=VMEM_LIMIT),
        cost_estimate=pl.CostEstimate(
            flops=rows * cols * keys * 4,
            bytes_accessed=keys * HD * 4 + rows * cols * 8,
            transcendentals=rows * (cols // HD) * keys,
        ),
        name="context_attention",
    )(q, key, value, old, old_stats)


def combine_kernel(parts_ref, out_ref):
    heads = out_ref.shape[2] // HD
    stats = parts_ref[:, :, heads * HD :].astype(F32)
    stats = (
        stats
        + pltpu.roll(stats, HD - N_HEAD, 2)
        + pltpu.roll(stats, HD - 2 * N_HEAD, 2)
    )
    factors = jnp.exp2(stats - jnp.max(stats, axis=0, keepdims=True))
    totals = pltpu.roll(stats, HD - 3 * N_HEAD, 2)
    share = factors / jnp.sum(totals * factors, axis=0, keepdims=True)
    for g in range(heads):
        cols = slice(g * HD, (g + 1) * HD)
        mixed = jnp.sum(parts_ref[:, :, cols].astype(F32) * share[:, :, g : g + 1], axis=0)
        out_ref[:, :, cols] = jnp.broadcast_to(
            mixed.astype(BF16)[None], out_ref.shape[:2] + (HD,)
        )


def combine(parts):
    groups, rows, cols = parts.shape
    return pl.pallas_call(
        combine_kernel,
        out_shape=jax.ShapeDtypeStruct((groups, rows, cols - HD), BF16),
        compiler_params=pltpu.CompilerParams(vmem_limit_bytes=VMEM_LIMIT),
        name="combine",
    )(parts)


def shift(value, axis, by):
    size = RING if axis != "core" else 2
    return lax.ppermute(value, axis, [(i, (i + by) % size) for i in range(size)])


def exchange(value, axis):
    return lax.all_to_all(value, axis, 0, 0, tiled=True)


def spread(value, axis, count):
    return exchange(jnp.broadcast_to(value[None], (count,) + value.shape), axis)


def body(
    fresh_states,
    query_states,
    w_query,
    w_key,
    w_value,
    w_output,
    cache_keys,
    cache_values,
    cached_mask,
    fresh_ids,
    anchor_id,
    query_pos,
):
    fresh_rows = fresh_states.shape[0]
    query_rows, width = query_states.shape
    depth, query_cols = w_query.shape
    held_blocks = cache_keys.shape[0]

    w_both = lax.all_gather(
        jnp.concatenate([w_key, w_value], axis=1), HST, axis=0, tiled=True
    )

    z, x, y, core = (lax.axis_index(a) for a in ("z", "x", "y", "core"))
    quarter = width // RING
    slab = quarter // N_HEAD
    steps = (1, -1, 2)
    slices = [
        lax.dynamic_slice_in_dim(
            fresh_states,
            lax.rem(z + d + RING, RING) * quarter + (y * 2 + core) * slab,
            slab,
            axis=1,
        )
        for d in steps
    ]
    owners = lax.rem(y + jnp.arange(RING, dtype=jnp.int32), RING) * 2
    at = jnp.concatenate([owners + core, owners + 1 - core]) * slab
    sources = jnp.stack([lax.rem(z - d + RING, RING) for d in steps])
    behind, ahead = shift(w_query, "x", 1), shift(w_query, "x", -1)
    middle = depth // 2
    turn = lax.rem(x + jnp.array([0, 1, 3, 2, 2], jnp.int32), RING) * depth
    turn = turn + jnp.array([0, 0, 0, 0, middle], jnp.int32)
    spots = jnp.concatenate([z[None], sources, at, turn])

    anchor = anchor_id[0]
    holder = lax.axis_index(HST) == anchor // held_blocks
    held = anchor % held_blocks
    anchor_parts = [
        jnp.where(holder, lax.dynamic_index_in_dim(a, held, 0, keepdims=False), 0).reshape(
            N_HST, -1, depth
        )
        for a in (cache_keys, cache_values)
    ]
    states = query_states.reshape(query_rows, N_HST, depth).transpose(1, 0, 2)
    packed = jnp.concatenate([states] + anchor_parts, axis=1)
    packed, slices = lax.optimization_barrier((packed, slices))
    mine = jnp.concatenate([shift(v, "z", d) for v, d in zip(slices, steps)], axis=0)
    got = exchange(packed, HST)
    got, mine = lax.optimization_barrier((got, mine))
    pieces = [mine, shift(mine, "y", -1), shift(mine, "y", 2), shift(mine, "y", 1)]
    own_anchor = jnp.sum(got[:, query_rows:].astype(F32), axis=0).astype(BF16)
    states = got[:, :query_rows].reshape(N_HST * query_rows, depth)

    partial = jnp.dot(states, w_query, preferred_element_type=F32).astype(BF16)
    partial, behind, ahead = lax.optimization_barrier((partial, behind, ahead))
    far = [shift(behind[:middle], "x", 1), shift(ahead[middle:], "x", -1)]
    partial = exchange(partial.reshape(N_HST, query_rows, query_cols), HST)
    query_cos, query_sin = rotary_tables(query_pos)
    own_queries = rotate(jnp.sum(partial.astype(F32), axis=0), query_cos, query_sin).astype(BF16)
    packed = jnp.concatenate([own_queries, own_anchor.reshape(-1, query_cols)], axis=0)
    packed = spread(packed, HST, N_HST)
    all_queries = packed[:, :query_rows].reshape(N_HST * query_rows, query_cols)
    anchors = packed[:, query_rows:].reshape(N_HST, 2, BLK // N_HST, HD)
    anchor_key = anchors[:, 0].reshape(BLK, HD)
    anchor_value = anchors[:, 1].reshape(BLK, HD)

    live = jnp.repeat(cached_mask == 1, BLK)
    bias = jnp.where(live, 0.0, DEAD).astype(F32)[None, :]
    weighted, stats = cached_attention(
        all_queries, cache_keys.reshape(-1, HD), cache_values.reshape(-1, HD), bias
    )

    places = (fresh_ids[:, None] * BLK + jnp.arange(BLK, dtype=jnp.int32)[None, :]).reshape(-1)
    cosine, sine = rotary_tables(places)
    fresh_key, fresh_value = key_value(fresh_states, w_both, cosine, sine)

    weighted, far, pieces = lax.optimization_barrier((weighted, far, pieces))
    pieces = pieces + [shift(piece, "core", 1) for piece in pieces]
    weights = [w_query, ahead, behind] + far
    sums = context_attention(all_queries, fresh_key, fresh_value, weighted, stats)
    spots, sums = lax.optimization_barrier((spots, sums))
    sums = exchange(sums.reshape(N_HST, query_rows, -1), HST)
    context = exchange(combine(sums), HST)
    product = jnp.dot(
        context.reshape(N_HST * query_rows, query_cols), w_output, preferred_element_type=F32
    )
    product = exchange(product.reshape(N_HEAD, -1, product.shape[1]), HEAD)
    query_output = jnp.sum(product, axis=0).astype(BF16)

    products = share_products(spots, fresh_states, pieces, weights)
    queries = lax.psum_scatter(
        products.reshape(-1, query_cols), "z", scatter_dimension=0, tiled=True
    )
    fresh_context = fresh_attention(
        [queries], (cosine, sine, fresh_key, fresh_value, anchor_key, anchor_value)
    )
    return fresh_context, query_output


def solution(mesh):
    mesh = Mesh(mesh.devices.reshape(RING, RING, RING, 2), HST + HEAD)
    return jax.shard_map(
        body,
        mesh=mesh,
        in_specs=(
            P(HST, None),
            P(HST, None),
            P(HST, HEAD),
            P(HST, HEAD),
            P(HST, HEAD),
            P(HEAD, HST),
            P(HST, None, HEAD),
            P(HST, None, HEAD),
            P(HST),
            P(HST),
            P(),
            P(HST),
        ),
        out_specs=(P(HST, HEAD), P(HEAD, HST)),
        check_vma=False,
    )
```

time: 221 us -> 187 us (0.85)
  waiting for transfers between devices: 95.2 us -> 45.8 us
  matrix products: 24.6 us -> 2.03 us
  Pallas kernels: 16.6 us -> 38.5 us
  starting transfers between devices: 23.2 us -> 40.8 us
  local copies, waits for them, and re-layouts: 2.55 us -> 14 us
  blocking collectives: 33.6 us -> 23 us
  other arithmetic: 9.95 us -> 6.78 us
    all_gather x2 -> x1, waiting for transfers between devices: 62.5 us -> 0.02 us  [body(): lax.all_gather(jnp.concatenate([w_key, w_value], axis=1), HST, axis=0, ti...]
    pallas_call x2 -> x6, Pallas kernels: 16.6 us -> 38.5 us  [the longest x1 13.8 us: share_products(): pl.pallas_call(functools.partial(shares_kernel, len(pieces)), grid_spec=p...]
    dot_general x2 -> x0, matrix products: 21.3 us -> none  [the longest x1 14.3 us: body(): query = jnp.dot(fresh_states, w_query_all, preferred_element_type=F32)]
    ppermute x0 -> x14, starting transfers between devices: none -> 20.5 us  [shift(): lax.ppermute(value, axis, [(i, (i + by) % size) for i in range(size)])]
    ppermute x0 -> x14, waiting for transfers between devices: none -> 16.9 us  [shift(): lax.ppermute(value, axis, [(i, (i + by) % size) for i in range(size)])]
    all_to_all x4, waiting for transfers between devices: 32 us -> 16.7 us  [exchange(): return lax.all_to_all(value, axis, 0, 0, tiled=True)]
    reduce_scatter x0 -> x1, waiting for transfers between devices: none -> 12.1 us  [body(): lax.psum_scatter(products.reshape(-1, query_cols), 'z', scatter_dimension...]
    all_to_all x2, blocking collectives: 33.6 us -> 23 us  [exchange(): return lax.all_to_all(value, axis, 0, 0, tiled=True)]
  transfers between devices with their start and end apart: 6 -> 20, of which waited for: 6 -> 9; matrix products, arithmetic and copies ran while one was open for 10% -> 8% of each run, Pallas kernels for 4% -> 10%
where the time goes in v2:
time: 187 us; the launch traced here: 186 us
  waiting for transfers between devices  45.8 us (24%)
  starting transfers between devices  40.8 us (22%)
  Pallas kernels  38.5 us (21%)
  blocking collectives  23 us (12%)
  between operations  15.1 us (8%)
  local copies, waits for them, and re-layouts  14 us (7%)
  other arithmetic  6.78 us (4%)
  matrix products  2.03 us (1%)
    all_to_all x2, blocking collectives, exchange(): return lax.all_to_all(value, axis, 0, 0, tiled=True)  23 us
    ppermute x14, starting transfers between devices, shift(): lax.ppermute(value, axis, [(i, (i + by) % size) for i in range(size)])  20.5 us
    all_to_all x4, starting transfers between devices, exchange(): return lax.all_to_all(value, axis, 0, 0, tiled=True)  20.2 us
    ppermute x14, waiting for transfers between devices, shift(): lax.ppermute(value, axis, [(i, (i + by) % size) for i in range(size)])  16.9 us
    all_to_all x4, waiting for transfers between devices, exchange(): return lax.all_to_all(value, axis, 0, 0, tiled=True)  16.7 us
    pallas_call x1, Pallas kernels, share_products(): pl.pallas_call(functools.partial(shares_kernel, len(pieces)), grid_spec=p...  13.8 us
    reduce_scatter x1, waiting for transfers between devices, body(): lax.psum_scatter(products.reshape(-1, query_cols), 'z', scatter_dimension...  12.1 us
    pallas_call x1, Pallas kernels, cached_attention(): pl.pallas_call(cached_kernel, grid=(cols // wide,), in_specs=[pl.BlockSpe...  7.91 us
  transfers between devices with their start and end apart: 20, of which 9 were waited for; matrix products, arithmetic and copies ran while one was open for 8% of the time, Pallas kernels for 10%

profile of v2, /device:TPU:1, one launch (start us, length us, event | category | flops | bytes accessed | tf_op | source)
XLA Modules:
  0.0 185.9 jit_solution(5866362345069046522)
XLA Ops:
  7.2 1.8 pad_maximum_fusion.2
  9.0 2.1 %collective-permute-start.3 = (bf16[512,1024]{1,0:T(8,128)(2,1)}, bf16[512,1024]{1,0:T(8,128)(2,1)}, u32[]{:S(2)}, u32[]{:S(2)}) collective-permute-start(bf16[512,1024]{1,0:T(8,128)(2,1)} %refs_8_.1), channel_id=1, source_target_pairs={{0,8},{8,16},{16,24},{24,0},{1,9},{9,17},{17,25},{25,1},{2,10},{10... | collective-permute-start | bytes 3145736 | tf_op jit(solution)/shard_map/ppermute | solution.py:374
  11.1 1.4 collective-permute-start.4
  13.2 0.9 dynamic-slice_select_fusion
  14.2 1.7 pad_maximum_fusion.1
  15.9 1.3 constant_dynamic-slice_fusion
  17.1 6.5 %all-to-all-start = ((bf16[16,16,512]{2,1,0:T(8,128)(2,1)}), bf16[16,16,512]{2,1,0:T(8,128)(2,1)S(1)}, u32[]{:S(2)}, u32[]{:S(2)}) async-start(bf16[16,16,512]{2,1,0:T(8,128)(2,1)} %pad_maximum_fusion.1), calls=%async_computation | async-start | bytes 524288 | tf_op jit(solution)/shard_map/all_to_all | solution.py:378
  23.7 1.4 collective-permute-start
  25.0 1.4 collective-permute-start.1
  26.4 1.6 collective-permute-start.2
  28.2 8.2 %collective-permute-done = bf16[512,256]{1,0:T(8,128)(2,1)S(1)} collective-permute-done((bf16[512,256]{1,0:T(8,128)(2,1)S(1)}, bf16[512,256]{1,0:T(8,128)(2,1)S(1)}, u32[]{:S(2)}, u32[]{:S(2)}) %collective-permute-start) | collective-permute-done | bytes 262176 | tf_op jit(solution)/shard_map/ppermute | solution.py:374
  36.5 7.0 %collective-permute-done.2 = bf16[512,256]{1,0:T(8,128)(2,1)S(1)} collective-permute-done((bf16[512,256]{1,0:T(8,128)(2,1)S(1)}, bf16[512,256]{1,0:T(8,128)(2,1)S(1)}, u32[]{:S(2)}, u32[]{:S(2)}) %collective-permute-start.2) | collective-permute-done | bytes 262176 | tf_op jit(solution)/shard_map/ppermute | solution.py:374
  43.6 3.0 %all-to-all-done = bf16[16,16,512]{2,1,0:T(8,128)(2,1)S(1)} async-done(((bf16[16,16,512]{2,1,0:T(8,128)(2,1)}), bf16[16,16,512]{2,1,0:T(8,128)(2,1)S(1)}, u32[]{:S(2)}, u32[]{:S(2)}) %all-to-all-start) | async-done | bytes 262176 | tf_op jit(solution)/shard_map/all_to_all | solution.py:378
  46.6 1.0 convolution_convert_fusion
  47.6 3.5 %all-to-all-start.1 = ((bf16[16,8,1024]{2,1,0:T(8,128)(2,1)}), bf16[16,8,1024]{2,1,0:T(8,128)(2,1)S(1)}, u32[]{:S(2)}, u32[]{:S(2)}) async-start(bf16[16,8,1024]{2,1,0:T(8,128)(2,1)} %bitcast.8), calls=%async_computation.1 | async-start | bytes 524288 | tf_op jit(solution)/shard_map/all_to_all | solution.py:378
  51.2 1.3 collective-permute-start.9
  52.6 2.6 %collective-permute-start.8 = (bf16[1536,256]{1,0:T(8,128)(2,1)S(1)}, bf16[1536,256]{1,0:T(8,128)(2,1)}, u32[]{:S(2)}, u32[]{:S(2)}) collective-permute-start(bf16[1536,256]{1,0:T(8,128)(2,1)S(1)} %pad_maximum_fusion.refs_0_), channel_id=1, source_target_pairs={{0,4},{2,6},{4,0},{6,2},{1,5},{3,7},{5,1},{7,3},{8,12},{10,14},{12... | collective-permute-start | bytes 2359304 | tf_op jit(solution)/shard_map/ppermute | solution.py:374
  55.2 1.1 collective-permute-start.7
  56.3 5.7 %all-to-all-done.1 = bf16[16,8,1024]{2,1,0:T(8,128)(2,1)S(1)} async-done(((bf16[16,8,1024]{2,1,0:T(8,128)(2,1)}), bf16[16,8,1024]{2,1,0:T(8,128)(2,1)S(1)}, u32[]{:S(2)}, u32[]{:S(2)}) %all-to-all-start.1) | async-done | bytes 262176 | tf_op jit(solution)/shard_map/all_to_all | solution.py:378
  62.2 0.8 broadcast_in_dim.36
  63.0 3.6 %all-to-all-start.2 = ((bf16[16,12,1024]{2,1,0:T(8,128)(2,1)}), bf16[16,12,1024]{2,1,0:T(8,128)(2,1)S(1)}, u32[]{:S(2)}, u32[]{:S(2)}) async-start(bf16[16,12,1024]{2,1,0:T(8,128)(2,1)} %broadcast_in_dim.36), calls=%async_computation.2 | async-start | bytes 1048576 | tf_op jit(solution)/shard_map/all_to_all | solution.py:378
  66.8 1.9 %slice.35 = bf16[256,1024]{1,0:T(8,128)(2,1)} slice(bf16[512,1024]{1,0:T(8,128)(2,1)} %collective-permute-done.3.refs_10_), slice={[0:256], [0:1024]} | slice | bytes 1048576 | tf_op jit(solution)/shard_map/slice | solution.py:451
  68.6 1.9 %slice.36 = bf16[256,1024]{1,0:T(8,128)(2,1)} slice(bf16[512,1024]{1,0:T(8,128)(2,1)} %collective-permute-done.4.refs_9_), slice={[256:512], [0:1024]} | slice | bytes 1048576 | tf_op jit(solution)/shard_map/slice | solution.py:451
  70.5 2.5 %collective-permute-start.6 = (bf16[256,1024]{1,0:T(8,128)(2,1)}, bf16[256,1024]{1,0:T(8,128)(2,1)S(1)}, u32[]{:S(2)}, u32[]{:S(2)}) collective-permute-start(bf16[256,1024]{1,0:T(8,128)(2,1)} %slice.36), channel_id=1, source_target_pairs={{0,24},{8,0},{16,8},{24,16},{1,25},{9,1},{17,9},{25,17},{2,26},{10... | collective-permute-start | bytes 1572872 | tf_op jit(solution)/shard_map/ppermute | solution.py:374
  73.1 2.6 %all-to-all-done.2 = bf16[16,12,1024]{2,1,0:T(8,128)(2,1)S(1)} async-done(((bf16[16,12,1024]{2,1,0:T(8,128)(2,1)}), bf16[16,12,1024]{2,1,0:T(8,128)(2,1)S(1)}, u32[]{:S(2)}, u32[]{:S(2)}) %all-to-all-start.2) | async-done | bytes 393248 | tf_op jit(solution)/shard_map/all_to_all | solution.py:378
  75.7 0.8 copy-done.11
  76.5 1.2 copy-done.6
  77.7 1.2 copy-done.7
  78.9 7.9 %cached_attention.1 = (f32[128,1024]{1,0:T(8,128)S(1)}, f32[128,128]{1,0:T(8,128)S(1)}) custom-call(bf16[128,1024]{1,0:T(8,128)(2,1)S(1)} %slice_bitcast_fusion.q_ref, bf16[4096,128]{1,0:T(8,128)(2,1)S(1)} %bitcast.53, bf16[4096,128]{1,0:T(8,128)(2,1)S(1)} %bitcast.52, f32[1,4096]{1,0:T(1,128)S(1)} %bitcast.51), custom_call_target="tpu_custom_call" | custom-call | flops 2147483648 | bytes 2621440 | tf_op jit(solution)/shard_map/cached_attention/pallas_call | solution.py:280
  87.1 1.4 collective-permute-done.7.refs_1_
  88.5 4.6 %collective-permute-start.10 = (bf16[1536,256]{1,0:T(8,128)(2,1)S(1)}, bf16[1536,256]{1,0:T(8,128)(2,1)}, u32[]{:S(2)}, u32[]{:S(2)}) collective-permute-start(bf16[1536,256]{1,0:T(8,128)(2,1)S(1)} %pad_maximum_fusion.refs_0_), channel_id=1, source_target_pairs={{0,1},{1,0},{2,3},{3,2},{4,5},{5,4},{6,7},{7,6},{8,9},{9,8},{10,11... | collective-permute-start | bytes 2359304 | tf_op jit(solution)/shard_map/ppermute | solution.py:374
  93.2 0.4 collective-permute-start.12
  93.8 1.0 fusion.4
  95.1 2.2 %copy-done.1 = bf16[8192,256]{1,0:T(8,128)(2,1)S(1)} copy-done((bf16[8192,256]{1,0:T(8,128)(2,1)S(1)}, bf16[8192,256]{1,0:T(8,128)(2,1)}, u32[]{:S(2)}) %copy-start.1) | copy-done | bytes 4194328
  97.3 7.6 %key_value.1 = (bf16[512,128]{1,0:T(8,128)(2,1)S(1)}, bf16[512,128]{1,0:T(8,128)(2,1)S(1)}) custom-call(bf16[512,8192]{1,0:T(8,128)(2,1)} %states_ref.3, bf16[8192,256]{1,0:T(8,128)(2,1)S(1)} %copy-done.1, f32[512,128]{1,0:T(8,128)S(1)} %get-tuple-element.65.cos_ref.refs_1_, f32[512,128]{1,0:T(8,128)S(1)} %get-tuple-element.66.sin_ref.refs_2_), custom_call_target="tpu_custom_call" | custom-call | flops 2147483648 | bytes 12582912 | tf_op jit(solution)/shard_map/key_value/pallas_call | solution.py:206
  104.9 2.2 %context_attention.1 = bf16[128,1152]{1,0:T(8,128)(2,1)S(1)} custom-call(bf16[128,1024]{1,0:T(8,128)(2,1)S(1)} %slice_bitcast_fusion.q_ref, bf16[512,128]{1,0:T(8,128)(2,1)S(1)} %get-tuple-element.30.k_ref.refs_3_, bf16[512,128]{1,0:T(8,128)(2,1)S(1)} %get-tuple-element.31.v_ref.refs_4_, f32[128,1024]{1,0:T(8,128)S(1)} %get-tuple-element.36.old_ref, ...), custom_call_target="tpu_custom_call" | custom-call | flops 268435456 | bytes 1310720 | tf_op jit(solution)/shard_map/context_attention/pallas_call | solution.py:330
  107.2 13.8 %share_products.1 = bf16[4,512,1024]{2,1,0:T(8,128)(2,1)} custom-call(s32[17]{0:T(128)S(1)} %concatenate.34.place_ref, bf16[512,8192]{1,0:T(8,128)(2,1)} %states_ref.3, bf16[1536,256]{1,0:T(8,128)(2,1)S(1)} %pad_maximum_fusion.refs_0_, bf16[1536,256]{1,0:T(8,128)(2,1)} %collective-permute-done.7.refs_1_, bf16[1536,256]{1,0:T(8,128)(2,1)} %collective-permute-done.8.refs_2_, ...), custom_call_target="tpu_custom_call" | custom-call | flops 8589934592 | bytes 16777216 | tf_op jit(solution)/shard_map/share_products/pallas_call | solution.py:156
  121.1 12.4 %all_to_all.30.parts_ref = bf16[16,8,1152]{2,1,0:T(8,128)(2,1)S(1)} all-to-all(bf16[16,8,1152]{2,1,0:T(8,128)(2,1)S(1)} %bitcast.48), channel_id=1, replica_groups=mesh['z'=4,'x'=4,'y'=4,'core'=2] {'z','x'}, dimensions={0} | all-to-all | bytes 589824 | tf_op jit(solution)/shard_map/all_to_all | solution.py:378
  133.5 0.4 combine.1
  133.9 10.5 %all_to_all.31 = bf16[16,8,1024]{2,1,0:T(8,128)(2,1)S(1)} all-to-all(bf16[16,8,1024]{2,1,0:T(8,128)(2,1)S(1)} %combine.1), channel_id=1, replica_groups=mesh['z'=4,'x'=4,'y'=4,'core'=2] {'z','x'}, dimensions={0} | all-to-all | bytes 524288 | tf_op jit(solution)/shard_map/all_to_all | solution.py:378
  144.5 1.0 fusion
  145.5 6.6 %all-to-all-start.5 = ((f32[8,16,512]{2,1,0:T(8,128)}), f32[8,16,512]{2,1,0:T(8,128)S(1)}, u32[]{:S(2)}, u32[]{:S(2)}) async-start(f32[8,16,512]{2,1,0:T(8,128)} %fusion), calls=%async_computation.6 | async-start | bytes 524288 | tf_op jit(solution)/shard_map/all_to_all | solution.py:378
  152.1 1.0 slice.43
  153.1 5.4 %all-to-all-done.5 = f32[8,16,512]{2,1,0:T(8,128)S(1)} async-done(((f32[8,16,512]{2,1,0:T(8,128)}), f32[8,16,512]{2,1,0:T(8,128)S(1)}, u32[]{:S(2)}, u32[]{:S(2)}) %all-to-all-start.5) | async-done | bytes 262176 | tf_op jit(solution)/shard_map/all_to_all | solution.py:378
  158.6 0.6 reduce_sum.32
  159.2 12.1 %reduce-scatter.2.cloned.1.call-done.refs_0_ = bf16[512,1024]{1,0:T(8,128)(2,1)} async-done(((bf16[2048,1024]{1,0:T(8,128)(2,1)}), bf16[512,1024]{1,0:T(8,128)(2,1)}) %reduce-scatter.2.cloned.1.call-update) | async-done | bytes 1048592 | tf_op jit(solution)/shard_map/reduce_scatter | solution.py:486
  171.3 1.2 copy-done.8
  172.6 6.5 %fresh_attention.1 = bf16[512,1024]{1,0:T(8,128)(2,1)} custom-call(bf16[512,1024]{1,0:T(8,128)(2,1)S(1)} %copy-done.8, f32[512,128]{1,0:T(8,128)S(1)} %get-tuple-element.65.cos_ref.refs_1_, f32[512,128]{1,0:T(8,128)S(1)} %get-tuple-element.66.sin_ref.refs_2_, bf16[512,128]{1,0:T(8,128)(2,1)S(1)} %copy-done.3, bf16[512,128]{1,0:T(8,128)(2,1)S(1)} %copy-done.5, ...), custom_call_target="tpu_custom_call" | custom-call | flops 1073741824 | bytes 2097152 | tf_op jit(solution)/shard_map/fresh_attention/pallas_call | solution.py:87
  (77 shorter events, 1.9 us)
Async XLA Ops:
  7.2 137.3 %copy-start = (bf16[1024,512]{1,0:T(8,128)(2,1)S(1)}, bf16[1024,512]{1,0:T(8,128)(2,1)}, u32[]{:S(2)}) copy-start(bf16[1024,512]{1,0:T(8,128)(2,1)} %param.19) | copy-start | bytes 3145732
  7.2 87.9 %all-gather.2.cloned.1.call-start = ((), (), s32[]{:S(2)}) async-start(), calls=%async_computation.7 | async-start | bytes 4456448 | tf_op jit(solution)/shard_map/all_gather | solution.py:404
  9.0 38.6 %collective-permute-start.3 = (bf16[512,1024]{1,0:T(8,128)(2,1)}, bf16[512,1024]{1,0:T(8,128)(2,1)}, u32[]{:S(2)}, u32[]{:S(2)}) collective-permute-start(bf16[512,1024]{1,0:T(8,128)(2,1)} %refs_8_.1), channel_id=1, source_target_pairs={{0,8},{8,16},{16,24},{24,0},{1,9},{9,17},{17,25},{25,1},{2,10},{10... | collective-permute-start | bytes 3145736 | tf_op jit(solution)/shard_map/ppermute | solution.py:374
  11.1 36.4 %collective-permute-start.4 = (bf16[512,1024]{1,0:T(8,128)(2,1)}, bf16[512,1024]{1,0:T(8,128)(2,1)}, u32[]{:S(2)}, u32[]{:S(2)}) collective-permute-start(bf16[512,1024]{1,0:T(8,128)(2,1)} %refs_8_.1), channel_id=1, source_target_pairs={{0,24},{8,0},{16,8},{24,16},{1,25},{9,1},{17,9},{25,17},{2,26},{10... | collective-permute-start | bytes 3145736 | tf_op jit(solution)/shard_map/ppermute | solution.py:374
  13.2 14.8 %copy-start.15 = (s32[2]{0:T(128)S(1)}, s32[2]{0:T(128)}, u32[]{:S(2)}) copy-start(s32[2]{0:T(128)} %param.23) | copy-start | bytes 28
  13.2 14.9 %copy-start.16 = (s32[8]{0:T(128)S(1)}, s32[8]{0:T(128)}, u32[]{:S(2)}) copy-start(s32[8]{0:T(128)} %param.25) | copy-start | bytes 100
  15.9 30.7 %copy-start.12 = (bf16[512,1024]{1,0:T(8,128)(2,1)S(1)}, bf16[512,1024]{1,0:T(8,128)(2,1)}, u32[]{:S(2)}) copy-start(bf16[512,1024]{1,0:T(8,128)(2,1)} %refs_8_.1) | copy-start | bytes 3145732
  17.1 29.4 %all-to-all-start = ((bf16[16,16,512]{2,1,0:T(8,128)(2,1)}), bf16[16,16,512]{2,1,0:T(8,128)(2,1)S(1)}, u32[]{:S(2)}, u32[]{:S(2)}) async-start(bf16[16,16,512]{2,1,0:T(8,128)(2,1)} %pad_maximum_fusion.1), calls=%async_computation | async-start | bytes 524288 | tf_op jit(solution)/shard_map/all_to_all | solution.py:378
  23.7 12.8 %collective-permute-start = (bf16[512,256]{1,0:T(8,128)(2,1)S(1)}, bf16[512,256]{1,0:T(8,128)(2,1)S(1)}, u32[]{:S(2)}, u32[]{:S(2)}) collective-permute-start(bf16[512,256]{1,0:T(8,128)(2,1)S(1)} %get-tuple-element.25), channel_id=1, source_target_pairs={{0,32},{32,64},{64,96},{96,0},{1,33},{33,65},{65,97},{97,1},{2,34}... | collective-permute-start | bytes 786440 | tf_op jit(solution)/shard_map/ppermute | solution.py:374
  25.0 11.5 %collective-permute-start.1 = (bf16[512,256]{1,0:T(8,128)(2,1)S(1)}, bf16[512,256]{1,0:T(8,128)(2,1)S(1)}, u32[]{:S(2)}, u32[]{:S(2)}) collective-permute-start(bf16[512,256]{1,0:T(8,128)(2,1)S(1)} %get-tuple-element.26), channel_id=1, source_target_pairs={{0,96},{32,0},{64,32},{96,64},{1,97},{33,1},{65,33},{97,65},{2,98}... | collective-permute-start | bytes 786440 | tf_op jit(solution)/shard_map/ppermute | solution.py:374
  26.4 17.1 %collective-permute-start.2 = (bf16[512,256]{1,0:T(8,128)(2,1)S(1)}, bf16[512,256]{1,0:T(8,128)(2,1)S(1)}, u32[]{:S(2)}, u32[]{:S(2)}) collective-permute-start(bf16[512,256]{1,0:T(8,128)(2,1)S(1)} %get-tuple-element.27), channel_id=1, source_target_pairs={{0,64},{32,96},{64,0},{96,32},{1,65},{33,97},{65,1},{97,33},{2,66}... | collective-permute-start | bytes 786440 | tf_op jit(solution)/shard_map/ppermute | solution.py:374
  28.2 22.9 %copy-start.17 = (s32[16]{0:T(128)S(1)}, s32[16]{0:T(128)}, u32[]{:S(2)}) copy-start(s32[16]{0:T(128)} %param.22) | copy-start | bytes 196
  47.6 14.4 %all-to-all-start.1 = ((bf16[16,8,1024]{2,1,0:T(8,128)(2,1)}), bf16[16,8,1024]{2,1,0:T(8,128)(2,1)S(1)}, u32[]{:S(2)}, u32[]{:S(2)}) async-start(bf16[16,8,1024]{2,1,0:T(8,128)(2,1)} %bitcast.8), calls=%async_computation.1 | async-start | bytes 524288 | tf_op jit(solution)/shard_map/all_to_all | solution.py:378
  51.2 35.6 %collective-permute-start.9 = (bf16[1536,256]{1,0:T(8,128)(2,1)S(1)}, bf16[1536,256]{1,0:T(8,128)(2,1)}, u32[]{:S(2)}, u32[]{:S(2)}) collective-permute-start(bf16[1536,256]{1,0:T(8,128)(2,1)S(1)} %pad_maximum_fusion.refs_0_), channel_id=1, source_target_pairs={{0,2},{2,4},{4,6},{6,0},{1,3},{3,5},{5,7},{7,1},{8,10},{10,12},{12... | collective-permute-start | bytes 2359304 | tf_op jit(solution)/shard_map/ppermute | solution.py:374
  52.6 34.6 %collective-permute-start.8 = (bf16[1536,256]{1,0:T(8,128)(2,1)S(1)}, bf16[1536,256]{1,0:T(8,128)(2,1)}, u32[]{:S(2)}, u32[]{:S(2)}) collective-permute-start(bf16[1536,256]{1,0:T(8,128)(2,1)S(1)} %pad_maximum_fusion.refs_0_), channel_id=1, source_target_pairs={{0,4},{2,6},{4,0},{6,2},{1,5},{3,7},{5,1},{7,3},{8,12},{10,14},{12... | collective-permute-start | bytes 2359304 | tf_op jit(solution)/shard_map/ppermute | solution.py:374
  55.2 33.3 %collective-permute-start.7 = (bf16[1536,256]{1,0:T(8,128)(2,1)S(1)}, bf16[1536,256]{1,0:T(8,128)(2,1)}, u32[]{:S(2)}, u32[]{:S(2)}) collective-permute-start(bf16[1536,256]{1,0:T(8,128)(2,1)S(1)} %pad_maximum_fusion.refs_0_), channel_id=1, source_target_pairs={{0,6},{2,0},{4,2},{6,4},{1,7},{3,1},{5,3},{7,5},{8,14},{10,8},{12,... | collective-permute-start | bytes 2359304 | tf_op jit(solution)/shard_map/ppermute | solution.py:374
  63.0 12.6 %all-to-all-start.2 = ((bf16[16,12,1024]{2,1,0:T(8,128)(2,1)}), bf16[16,12,1024]{2,1,0:T(8,128)(2,1)S(1)}, u32[]{:S(2)}, u32[]{:S(2)}) async-start(bf16[16,12,1024]{2,1,0:T(8,128)(2,1)} %broadcast_in_dim.36), calls=%async_computation.2 | async-start | bytes 1048576 | tf_op jit(solution)/shard_map/all_to_all | solution.py:378
  66.6 104.7 %reduce-scatter.2.cloned.1.call-start = ((), (), s32[]{:S(2)}) async-start(), calls=%async_computation.8 | async-start | bytes 5242880 | tf_op jit(solution)/shard_map/reduce_scatter | solution.py:486
  70.5 18.0 %collective-permute-start.6 = (bf16[256,1024]{1,0:T(8,128)(2,1)}, bf16[256,1024]{1,0:T(8,128)(2,1)S(1)}, u32[]{:S(2)}, u32[]{:S(2)}) collective-permute-start(bf16[256,1024]{1,0:T(8,128)(2,1)} %slice.36), channel_id=1, source_target_pairs={{0,24},{8,0},{16,8},{24,16},{1,25},{9,1},{17,9},{25,17},{2,26},{10... | collective-permute-start | bytes 1572872 | tf_op jit(solution)/shard_map/ppermute | solution.py:374
  73.0 15.5 %collective-permute-start.5 = (bf16[256,1024]{1,0:T(8,128)(2,1)}, bf16[256,1024]{1,0:T(8,128)(2,1)}, u32[]{:S(2)}, u32[]{:S(2)}) collective-permute-start(bf16[256,1024]{1,0:T(8,128)(2,1)} %slice.35), channel_id=1, source_target_pairs={{0,8},{8,16},{16,24},{24,0},{1,9},{9,17},{17,25},{25,1},{2,10},{10... | collective-permute-start | bytes 1572872 | tf_op jit(solution)/shard_map/ppermute | solution.py:374
  75.7 0.8 copy-start.11
  76.5 1.2 copy-start.6
  77.7 1.2 copy-start.7
  78.9 14.8 %copy-start.13 = (s32[5]{0:T(128)S(1)}, s32[5]{0:T(128)}, u32[]{:S(2)}) copy-start(s32[5]{0:T(128)} %constant.127.clone) | copy-start | bytes 64
  78.9 14.8 %copy-start.14 = (s32[5]{0:T(128)S(1)}, s32[5]{0:T(128)}, u32[]{:S(2)}) copy-start(s32[5]{0:T(128)} %constant.126.clone) | copy-start | bytes 64
  88.5 6.3 %copy-start.9 = (bf16[256,1024]{1,0:T(8,128)(2,1)}, bf16[256,1024]{1,0:T(8,128)(2,1)S(1)}, u32[]{:S(2)}) copy-start(bf16[256,1024]{1,0:T(8,128)(2,1)S(1)} %collective-permute-done.6.refs_12_) | copy-start | bytes 1572868
  88.5 18.7 %collective-permute-start.10 = (bf16[1536,256]{1,0:T(8,128)(2,1)S(1)}, bf16[1536,256]{1,0:T(8,128)(2,1)}, u32[]{:S(2)}, u32[]{:S(2)}) collective-permute-start(bf16[1536,256]{1,0:T(8,128)(2,1)S(1)} %pad_maximum_fusion.refs_0_), channel_id=1, source_target_pairs={{0,1},{1,0},{2,3},{3,2},{4,5},{5,4},{6,7},{7,6},{8,9},{9,8},{10,11... | collective-permute-start | bytes 2359304 | tf_op jit(solution)/shard_map/ppermute | solution.py:374
  93.1 14.1 %collective-permute-start.11 = (bf16[1536,256]{1,0:T(8,128)(2,1)}, bf16[1536,256]{1,0:T(8,128)(2,1)}, u32[]{:S(2)}, u32[]{:S(2)}) collective-permute-start(bf16[1536,256]{1,0:T(8,128)(2,1)} %collective-permute-done.7.refs_1_), channel_id=1, source_target_pairs={{0,1},{1,0},{2,3},{3,2},{4,5},{5,4},{6,7},{7,6},{8,9},{9,8},{10,11... | collective-permute-start | bytes 2359304 | tf_op jit(solution)/shard_map/ppermute | solution.py:374
  93.2 14.0 %collective-permute-start.12 = (bf16[1536,256]{1,0:T(8,128)(2,1)}, bf16[1536,256]{1,0:T(8,128)(2,1)}, u32[]{:S(2)}, u32[]{:S(2)}) collective-permute-start(bf16[1536,256]{1,0:T(8,128)(2,1)} %collective-permute-done.8.refs_2_), channel_id=1, source_target_pairs={{0,1},{1,0},{2,3},{3,2},{4,5},{5,4},{6,7},{7,6},{8,9},{9,8},{10,11... | collective-permute-start | bytes 2359304 | tf_op jit(solution)/shard_map/ppermute | solution.py:374
  93.6 13.6 %collective-permute-start.13 = (bf16[1536,256]{1,0:T(8,128)(2,1)}, bf16[1536,256]{1,0:T(8,128)(2,1)}, u32[]{:S(2)}, u32[]{:S(2)}) collective-permute-start(bf16[1536,256]{1,0:T(8,128)(2,1)} %collective-permute-done.9.refs_3_), channel_id=1, source_target_pairs={{0,1},{1,0},{2,3},{3,2},{4,5},{5,4},{6,7},{7,6},{8,9},{9,8},{10,11... | collective-permute-start | bytes 2359304 | tf_op jit(solution)/shard_map/ppermute | solution.py:374
  95.1 2.2 %copy-start.1 = (bf16[8192,256]{1,0:T(8,128)(2,1)S(1)}, bf16[8192,256]{1,0:T(8,128)(2,1)}, u32[]{:S(2)}) copy-start(bf16[8192,256]{1,0:T(8,128)(2,1)} %all-gather.2.cloned.1.call-done.w_ref) | copy-start | bytes 12582916
  97.3 10.0 %copy-start.10 = (bf16[256,1024]{1,0:T(8,128)(2,1)S(1)}, bf16[256,1024]{1,0:T(8,128)(2,1)}, u32[]{:S(2)}) copy-start(bf16[256,1024]{1,0:T(8,128)(2,1)} %copy-done.9) | copy-start | bytes 1572868
  104.9 2.3 %copy-start.2 = (bf16[512,128]{1,0:T(8,128)(2,1)}, bf16[512,128]{1,0:T(8,128)(2,1)S(1)}, u32[]{:S(2)}) copy-start(bf16[512,128]{1,0:T(8,128)(2,1)S(1)} %get-tuple-element.30.k_ref.refs_3_) | copy-start | bytes 393220
  104.9 2.3 %copy-start.4 = (bf16[512,128]{1,0:T(8,128)(2,1)}, bf16[512,128]{1,0:T(8,128)(2,1)S(1)}, u32[]{:S(2)}) copy-start(bf16[512,128]{1,0:T(8,128)(2,1)S(1)} %get-tuple-element.31.v_ref.refs_4_) | copy-start | bytes 393220
  144.4 26.9 %copy-start.3 = (bf16[512,128]{1,0:T(8,128)(2,1)S(1)}, bf16[512,128]{1,0:T(8,128)(2,1)}, u32[]{:S(2)}) copy-start(bf16[512,128]{1,0:T(8,128)(2,1)} %copy-done.2) | copy-start | bytes 393220
  144.4 26.9 %copy-start.5 = (bf16[512,128]{1,0:T(8,128)(2,1)S(1)}, bf16[512,128]{1,0:T(8,128)(2,1)}, u32[]{:S(2)}) copy-start(bf16[512,128]{1,0:T(8,128)(2,1)} %copy-done.4) | copy-start | bytes 393220
  145.5 13.1 %all-to-all-start.5 = ((f32[8,16,512]{2,1,0:T(8,128)}), f32[8,16,512]{2,1,0:T(8,128)S(1)}, u32[]{:S(2)}, u32[]{:S(2)}) async-start(f32[8,16,512]{2,1,0:T(8,128)} %fusion), calls=%async_computation.6 | async-start | bytes 524288 | tf_op jit(solution)/shard_map/all_to_all | solution.py:378
  171.3 1.2 copy-start.8
Sparse Core Ops, SparseCore 0:
  10.2 60.1 all-gather.1
  121.2 50.0 reduce-scatter.1

commit v3 on v2

--- a/solution.py
+++ b/solution.py
@@ -200,7 +200,7 @@
 
 def key_value(states, weights, cosine, sine):
     rows, depth = states.shape
-    step = 1024
+    step = 2048
     whole = lambda a: pl.BlockSpec(a.shape, lambda i: (0, 0))
     out = jax.ShapeDtypeStruct((rows, HD), BF16)
     return pl.pallas_call(
@@ -469,11 +469,10 @@
     cosine, sine = rotary_tables(places)
     fresh_key, fresh_value = key_value(fresh_states, w_both, cosine, sine)
 
-    weighted, far, pieces = lax.optimization_barrier((weighted, far, pieces))
+    weighted, far, pieces, spots = lax.optimization_barrier((weighted, far, pieces, spots))
     pieces = pieces + [shift(piece, "core", 1) for piece in pieces]
     weights = [w_query, ahead, behind] + far
     sums = context_attention(all_queries, fresh_key, fresh_value, weighted, stats)
-    spots, sums = lax.optimization_barrier((spots, sums))
     sums = exchange(sums.reshape(N_HST, query_rows, -1), HST)
     context = exchange(combine(sums), HST)
     product = jnp.dot(

time: 187 us -> 182 us (0.973)
  waiting for transfers between devices: 45.8 us -> 41.7 us
    reduce_scatter x1, waiting for transfers between devices: 12.1 us -> 0.04 us  [body(): lax.psum_scatter(products.reshape(-1, query_cols), 'z', scatter_dimension...]
    all_to_all x4, waiting for transfers between devices: 16.7 us -> 21.3 us  [exchange(): return lax.all_to_all(value, axis, 0, 0, tiled=True)]
    ppermute x14, waiting for transfers between devices: 16.9 us -> 20.3 us  [shift(): lax.ppermute(value, axis, [(i, (i + by) % size) for i in range(size)])]
    unnamed x39 -> x29, local copies, waits for them, and re-layouts: 6.81 us -> 7.49 us
  transfers between devices with their start and end apart: 20 -> 20, of which waited for: 9 -> 10; matrix products, arithmetic and copies ran while one was open for 8% -> 7% of each run, Pallas kernels for 10% -> 17%
where the time goes in v3:
time: 182 us; the launch traced here: 181 us
  waiting for transfers between devices  41.7 us (23%)
  starting transfers between devices  39.4 us (22%)
  Pallas kernels  37 us (20%)
  blocking collectives  23.7 us (13%)
  between operations  16.5 us (9%)
  local copies, waits for them, and re-layouts  13.7 us (8%)
  other arithmetic  6.79 us (4%)
  matrix products  2.03 us (1%)
    all_to_all x2, blocking collectives, exchange(): return lax.all_to_all(value, axis, 0, 0, tiled=True)  23.7 us
    all_to_all x4, waiting for transfers between devices, exchange(): return lax.all_to_all(value, axis, 0, 0, tiled=True)  21.3 us
    ppermute x14, waiting for transfers between devices, shift(): lax.ppermute(value, axis, [(i, (i + by) % size) for i in range(size)])  20.3 us
    all_to_all x4, starting transfers between devices, exchange(): return lax.all_to_all(value, axis, 0, 0, tiled=True)  19.7 us
    ppermute x14, starting transfers between devices, shift(): lax.ppermute(value, axis, [(i, (i + by) % size) for i in range(size)])  19.6 us
    pallas_call x1, Pallas kernels, share_products(): pl.pallas_call(functools.partial(shares_kernel, len(pieces)), grid_spec=p...  13.9 us
    pallas_call x1, Pallas kernels, cached_attention(): pl.pallas_call(cached_kernel, grid=(cols // wide,), in_specs=[pl.BlockSpe...  7.94 us
    unnamed x29, local copies, waits for them, and re-layouts  7.49 us
  transfers between devices with their start and end apart: 20, of which 10 were waited for; matrix products, arithmetic and copies ran while one was open for 7% of the time, Pallas kernels for 17%

profile of v3, /device:TPU:1, one launch (start us, length us, event | category | flops | bytes accessed | tf_op | source)
XLA Modules:
  0.0 180.8 jit_solution(3010494261382711062)
XLA Ops:
  8.1 1.8 pad_maximum_fusion.4
  9.9 2.1 %collective-permute-start.3 = (bf16[512,1024]{1,0:T(8,128)(2,1)}, bf16[512,1024]{1,0:T(8,128)(2,1)}, u32[]{:S(2)}, u32[]{:S(2)}) collective-permute-start(bf16[512,1024]{1,0:T(8,128)(2,1)} %refs_8_.1), channel_id=1, source_target_pairs={{0,8},{8,16},{16,24},{24,0},{1,9},{9,17},{17,25},{25,1},{2,10},{10... | collective-permute-start | bytes 3145736 | tf_op jit(solution)/shard_map/ppermute | solution.py:374
  12.0 1.4 collective-permute-start.4
  14.0 0.9 dynamic-slice_select_fusion
  15.0 1.7 pad_maximum_fusion.1
  16.7 1.3 constant_dynamic-slice_fusion
  18.0 6.5 %all-to-all-start = ((bf16[16,16,512]{2,1,0:T(8,128)(2,1)}), bf16[16,16,512]{2,1,0:T(8,128)(2,1)S(1)}, u32[]{:S(2)}, u32[]{:S(2)}) async-start(bf16[16,16,512]{2,1,0:T(8,128)(2,1)} %pad_maximum_fusion.1), calls=%async_computation | async-start | bytes 524288 | tf_op jit(solution)/shard_map/all_to_all | solution.py:378
  24.5 1.4 collective-permute-start
  25.9 1.4 collective-permute-start.1
  27.2 1.6 collective-permute-start.2
  29.0 8.2 %collective-permute-done = bf16[512,256]{1,0:T(8,128)(2,1)S(1)} collective-permute-done((bf16[512,256]{1,0:T(8,128)(2,1)S(1)}, bf16[512,256]{1,0:T(8,128)(2,1)S(1)}, u32[]{:S(2)}, u32[]{:S(2)}) %collective-permute-start) | collective-permute-done | bytes 262176 | tf_op jit(solution)/shard_map/ppermute | solution.py:374
  37.2 7.2 %collective-permute-done.2 = bf16[512,256]{1,0:T(8,128)(2,1)S(1)} collective-permute-done((bf16[512,256]{1,0:T(8,128)(2,1)S(1)}, bf16[512,256]{1,0:T(8,128)(2,1)S(1)}, u32[]{:S(2)}, u32[]{:S(2)}) %collective-permute-start.2) | collective-permute-done | bytes 262176 | tf_op jit(solution)/shard_map/ppermute | solution.py:374
  44.4 3.0 %all-to-all-done = bf16[16,16,512]{2,1,0:T(8,128)(2,1)S(1)} async-done(((bf16[16,16,512]{2,1,0:T(8,128)(2,1)}), bf16[16,16,512]{2,1,0:T(8,128)(2,1)S(1)}, u32[]{:S(2)}, u32[]{:S(2)}) %all-to-all-start) | async-done | bytes 262176 | tf_op jit(solution)/shard_map/all_to_all | solution.py:378
  47.4 1.0 convolution_convert_fusion
  48.4 3.7 %all-to-all-start.1 = ((bf16[16,8,1024]{2,1,0:T(8,128)(2,1)}), bf16[16,8,1024]{2,1,0:T(8,128)(2,1)S(1)}, u32[]{:S(2)}, u32[]{:S(2)}) async-start(bf16[16,8,1024]{2,1,0:T(8,128)(2,1)} %bitcast.4), calls=%async_computation.1 | async-start | bytes 524288 | tf_op jit(solution)/shard_map/all_to_all | solution.py:378
  52.3 1.3 collective-permute-start.9
  53.6 2.6 %collective-permute-start.8 = (bf16[1536,256]{1,0:T(8,128)(2,1)S(1)}, bf16[1536,256]{1,0:T(8,128)(2,1)}, u32[]{:S(2)}, u32[]{:S(2)}) collective-permute-start(bf16[1536,256]{1,0:T(8,128)(2,1)S(1)} %pad_maximum_fusion.refs_0_), channel_id=1, source_target_pairs={{0,4},{2,6},{4,0},{6,2},{1,5},{3,7},{5,1},{7,3},{8,12},{10,14},{12... | collective-permute-start | bytes 2359304 | tf_op jit(solution)/shard_map/ppermute | solution.py:374
  56.2 1.1 collective-permute-start.7
  57.4 5.6 %all-to-all-done.1 = bf16[16,8,1024]{2,1,0:T(8,128)(2,1)S(1)} async-done(((bf16[16,8,1024]{2,1,0:T(8,128)(2,1)}), bf16[16,8,1024]{2,1,0:T(8,128)(2,1)S(1)}, u32[]{:S(2)}, u32[]{:S(2)}) %all-to-all-start.1) | async-done | bytes 262176 | tf_op jit(solution)/shard_map/all_to_all | solution.py:378
  63.2 0.8 broadcast_in_dim.20
  64.0 3.6 %all-to-all-start.2 = ((bf16[16,12,1024]{2,1,0:T(8,128)(2,1)}), bf16[16,12,1024]{2,1,0:T(8,128)(2,1)S(1)}, u32[]{:S(2)}, u32[]{:S(2)}) async-start(bf16[16,12,1024]{2,1,0:T(8,128)(2,1)} %broadcast_in_dim.20), calls=%async_computation.2 | async-start | bytes 1048576 | tf_op jit(solution)/shard_map/all_to_all | solution.py:378
  67.8 1.9 %slice.35 = bf16[256,1024]{1,0:T(8,128)(2,1)} slice(bf16[512,1024]{1,0:T(8,128)(2,1)} %collective-permute-done.3.refs_10_), slice={[0:256], [0:1024]} | slice | bytes 1048576 | tf_op jit(solution)/shard_map/slice | solution.py:451
  69.6 1.9 %slice.36 = bf16[256,1024]{1,0:T(8,128)(2,1)} slice(bf16[512,1024]{1,0:T(8,128)(2,1)} %collective-permute-done.4.refs_9_), slice={[256:512], [0:1024]} | slice | bytes 1048576 | tf_op jit(solution)/shard_map/slice | solution.py:451
  71.5 2.5 %collective-permute-start.6 = (bf16[256,1024]{1,0:T(8,128)(2,1)}, bf16[256,1024]{1,0:T(8,128)(2,1)}, u32[]{:S(2)}, u32[]{:S(2)}) collective-permute-start(bf16[256,1024]{1,0:T(8,128)(2,1)} %slice.36), channel_id=1, source_target_pairs={{0,24},{8,0},{16,8},{24,16},{1,25},{9,1},{17,9},{25,17},{2,26},{10... | collective-permute-start | bytes 1572872 | tf_op jit(solution)/shard_map/ppermute | solution.py:374
  74.1 6.3 %all-to-all-done.2 = bf16[16,12,1024]{2,1,0:T(8,128)(2,1)S(1)} async-done(((bf16[16,12,1024]{2,1,0:T(8,128)(2,1)}), bf16[16,12,1024]{2,1,0:T(8,128)(2,1)S(1)}, u32[]{:S(2)}, u32[]{:S(2)}) %all-to-all-start.2) | async-done | bytes 393248 | tf_op jit(solution)/shard_map/all_to_all | solution.py:378
  80.5 1.2 copy-done.2
  81.7 1.2 copy-done.3
  82.9 7.9 %cached_attention.1 = (f32[128,1024]{1,0:T(8,128)S(1)}, f32[128,128]{1,0:T(8,128)S(1)}) custom-call(bf16[128,1024]{1,0:T(8,128)(2,1)S(1)} %slice_bitcast_fusion.q_ref, bf16[4096,128]{1,0:T(8,128)(2,1)S(1)} %bitcast.57, bf16[4096,128]{1,0:T(8,128)(2,1)S(1)} %bitcast.56, f32[1,4096]{1,0:T(1,128)S(1)} %bitcast.55), custom_call_target="tpu_custom_call" | custom-call | flops 2147483648 | bytes 2621440 | tf_op jit(solution)/shard_map/cached_attention/pallas_call | solution.py:280
  90.9 3.7 %collective-permute-start.10 = (bf16[1536,256]{1,0:T(8,128)(2,1)S(1)}, bf16[1536,256]{1,0:T(8,128)(2,1)S(1)}, u32[]{:S(2)}, u32[]{:S(2)}) collective-permute-start(bf16[1536,256]{1,0:T(8,128)(2,1)S(1)} %pad_maximum_fusion.refs_0_), channel_id=1, source_target_pairs={{0,1},{1,0},{2,3},{3,2},{4,5},{5,4},{6,7},{7,6},{8,9},{9,8},{10,11... | collective-permute-start | bytes 2359304 | tf_op jit(solution)/shard_map/ppermute | solution.py:374
  95.2 1.5 collective-permute-done.10.refs_4_
  96.7 1.1 collective-permute-done.11.refs_5_
  97.9 1.1 collective-permute-done.12.refs_6_
  99.0 1.1 collective-permute-done.13.refs_7_
  100.1 0.9 copy-done.9
  101.0 13.9 %share_products.1 = bf16[4,512,1024]{2,1,0:T(8,128)(2,1)} custom-call(s32[17]{0:T(128)S(1)} %concatenate.40.place_ref, bf16[512,8192]{1,0:T(8,128)(2,1)} %states_ref.3, bf16[1536,256]{1,0:T(8,128)(2,1)S(1)} %pad_maximum_fusion.refs_0_, bf16[1536,256]{1,0:T(8,128)(2,1)} %collective-permute-done.7.refs_1_, bf16[1536,256]{1,0:T(8,128)(2,1)} %collective-permute-done.8.refs_2_, ...), custom_call_target="tpu_custom_call" | custom-call | flops 8589934592 | bytes 16777216 | tf_op jit(solution)/shard_map/share_products/pallas_call | solution.py:156
  115.0 0.6 copy-done.12
  115.7 1.0 fusion.4
  117.0 2.2 %copy-done.1 = bf16[8192,256]{1,0:T(8,128)(2,1)S(1)} copy-done((bf16[8192,256]{1,0:T(8,128)(2,1)S(1)}, bf16[8192,256]{1,0:T(8,128)(2,1)}, u32[]{:S(2)}) %copy-start.1) | copy-done | bytes 4194328
  119.2 5.9 %key_value.1 = (bf16[512,128]{1,0:T(8,128)(2,1)S(1)}, bf16[512,128]{1,0:T(8,128)(2,1)S(1)}) custom-call(bf16[512,8192]{1,0:T(8,128)(2,1)} %states_ref.3, bf16[8192,256]{1,0:T(8,128)(2,1)S(1)} %copy-done.1, f32[512,128]{1,0:T(8,128)S(1)} %get-tuple-element.63.cos_ref.refs_1_, f32[512,128]{1,0:T(8,128)S(1)} %get-tuple-element.64.sin_ref.refs_2_), custom_call_target="tpu_custom_call" | custom-call | flops 2147483648 | bytes 12582912 | tf_op jit(solution)/shard_map/key_value/pallas_call | solution.py:206
  125.1 2.3 %context_attention.1 = bf16[128,1152]{1,0:T(8,128)(2,1)S(1)} custom-call(bf16[128,1024]{1,0:T(8,128)(2,1)S(1)} %slice_bitcast_fusion.q_ref, bf16[512,128]{1,0:T(8,128)(2,1)S(1)} %get-tuple-element.40.refs_3_.k_ref, bf16[512,128]{1,0:T(8,128)(2,1)S(1)} %get-tuple-element.41.refs_4_.v_ref, f32[128,1024]{1,0:T(8,128)S(1)} %get-tuple-element.42.old_ref, ...), custom_call_target="tpu_custom_call" | custom-call | flops 268435456 | bytes 1310720 | tf_op jit(solution)/shard_map/context_attention/pallas_call | solution.py:330
  127.3 11.8 %all_to_all.30.parts_ref = bf16[16,8,1152]{2,1,0:T(8,128)(2,1)S(1)} all-to-all(bf16[16,8,1152]{2,1,0:T(8,128)(2,1)S(1)} %bitcast.52), channel_id=1, replica_groups=mesh['z'=4,'x'=4,'y'=4,'core'=2] {'z','x'}, dimensions={0} | all-to-all | bytes 589824 | tf_op jit(solution)/shard_map/all_to_all | solution.py:378
  139.6 11.8 %all_to_all.31 = bf16[16,8,1024]{2,1,0:T(8,128)(2,1)S(1)} all-to-all(bf16[16,8,1024]{2,1,0:T(8,128)(2,1)S(1)} %combine.1), channel_id=1, replica_groups=mesh['z'=4,'x'=4,'y'=4,'core'=2] {'z','x'}, dimensions={0} | all-to-all | bytes 524288 | tf_op jit(solution)/shard_map/all_to_all | solution.py:378
  151.4 1.0 fusion
  152.4 6.0 %all-to-all-start.5 = ((f32[8,16,512]{2,1,0:T(8,128)}), f32[8,16,512]{2,1,0:T(8,128)S(1)}, u32[]{:S(2)}, u32[]{:S(2)}) async-start(f32[8,16,512]{2,1,0:T(8,128)} %fusion), calls=%async_computation.6 | async-start | bytes 524288 | tf_op jit(solution)/shard_map/all_to_all | solution.py:378
  158.5 6.4 %all-to-all-done.5 = f32[8,16,512]{2,1,0:T(8,128)S(1)} async-done(((f32[8,16,512]{2,1,0:T(8,128)}), f32[8,16,512]{2,1,0:T(8,128)S(1)}, u32[]{:S(2)}, u32[]{:S(2)}) %all-to-all-start.5) | async-done | bytes 262176 | tf_op jit(solution)/shard_map/all_to_all | solution.py:378
  164.9 0.6 reduce_sum.32
  165.6 1.2 copy-done.4
  166.8 6.5 %fresh_attention.1 = bf16[512,1024]{1,0:T(8,128)(2,1)} custom-call(bf16[512,1024]{1,0:T(8,128)(2,1)S(1)} %copy-done.4, f32[512,128]{1,0:T(8,128)S(1)} %get-tuple-element.63.cos_ref.refs_1_, f32[512,128]{1,0:T(8,128)S(1)} %get-tuple-element.64.sin_ref.refs_2_, bf16[512,128]{1,0:T(8,128)(2,1)S(1)} %get-tuple-element.40.refs_3_.k_ref, ...), custom_call_target="tpu_custom_call" | custom-call | flops 1073741824 | bytes 2097152 | tf_op jit(solution)/shard_map/fresh_attention/pallas_call | solution.py:87
  (67 shorter events, 2.5 us)
Async XLA Ops:
  8.0 143.4 %copy-start = (bf16[1024,512]{1,0:T(8,128)(2,1)S(1)}, bf16[1024,512]{1,0:T(8,128)(2,1)}, u32[]{:S(2)}) copy-start(bf16[1024,512]{1,0:T(8,128)(2,1)} %param.19) | copy-start | bytes 3145732
  8.0 108.9 %all-gather.2.cloned.1.call-start = ((), (), s32[]{:S(2)}) async-start(), calls=%async_computation.8 | async-start | bytes 4456448 | tf_op jit(solution)/shard_map/all_gather | solution.py:404
  9.9 38.6 %collective-permute-start.3 = (bf16[512,1024]{1,0:T(8,128)(2,1)}, bf16[512,1024]{1,0:T(8,128)(2,1)}, u32[]{:S(2)}, u32[]{:S(2)}) collective-permute-start(bf16[512,1024]{1,0:T(8,128)(2,1)} %refs_8_.1), channel_id=1, source_target_pairs={{0,8},{8,16},{16,24},{24,0},{1,9},{9,17},{17,25},{25,1},{2,10},{10... | collective-permute-start | bytes 3145736 | tf_op jit(solution)/shard_map/ppermute | solution.py:374
  12.0 36.5 %collective-permute-start.4 = (bf16[512,1024]{1,0:T(8,128)(2,1)}, bf16[512,1024]{1,0:T(8,128)(2,1)}, u32[]{:S(2)}, u32[]{:S(2)}) collective-permute-start(bf16[512,1024]{1,0:T(8,128)(2,1)} %refs_8_.1), channel_id=1, source_target_pairs={{0,24},{8,0},{16,8},{24,16},{1,25},{9,1},{17,9},{25,17},{2,26},{10... | collective-permute-start | bytes 3145736 | tf_op jit(solution)/shard_map/ppermute | solution.py:374
  14.0 14.8 %copy-start.10 = (s32[16]{0:T(128)S(1)}, s32[16]{0:T(128)}, u32[]{:S(2)}) copy-start(s32[16]{0:T(128)} %param.22) | copy-start | bytes 196
  14.0 14.8 %copy-start.11 = (s32[8]{0:T(128)S(1)}, s32[8]{0:T(128)}, u32[]{:S(2)}) copy-start(s32[8]{0:T(128)} %param.25) | copy-start | bytes 100
  16.7 30.7 %copy-start.5 = (bf16[512,1024]{1,0:T(8,128)(2,1)S(1)}, bf16[512,1024]{1,0:T(8,128)(2,1)}, u32[]{:S(2)}) copy-start(bf16[512,1024]{1,0:T(8,128)(2,1)} %refs_8_.1) | copy-start | bytes 3145732
  18.0 29.4 %all-to-all-start = ((bf16[16,16,512]{2,1,0:T(8,128)(2,1)}), bf16[16,16,512]{2,1,0:T(8,128)(2,1)S(1)}, u32[]{:S(2)}, u32[]{:S(2)}) async-start(bf16[16,16,512]{2,1,0:T(8,128)(2,1)} %pad_maximum_fusion.1), calls=%async_computation | async-start | bytes 524288 | tf_op jit(solution)/shard_map/all_to_all | solution.py:378
  24.5 12.7 %collective-permute-start = (bf16[512,256]{1,0:T(8,128)(2,1)S(1)}, bf16[512,256]{1,0:T(8,128)(2,1)S(1)}, u32[]{:S(2)}, u32[]{:S(2)}) collective-permute-start(bf16[512,256]{1,0:T(8,128)(2,1)S(1)} %get-tuple-element.24), channel_id=1, source_target_pairs={{0,32},{32,64},{64,96},{96,0},{1,33},{33,65},{65,97},{97,1},{2,34}... | collective-permute-start | bytes 786440 | tf_op jit(solution)/shard_map/ppermute | solution.py:374
  25.9 11.3 %collective-permute-start.1 = (bf16[512,256]{1,0:T(8,128)(2,1)S(1)}, bf16[512,256]{1,0:T(8,128)(2,1)S(1)}, u32[]{:S(2)}, u32[]{:S(2)}) collective-permute-start(bf16[512,256]{1,0:T(8,128)(2,1)S(1)} %get-tuple-element.25), channel_id=1, source_target_pairs={{0,96},{32,0},{64,32},{96,64},{1,97},{33,1},{65,33},{97,65},{2,98}... | collective-permute-start | bytes 786440 | tf_op jit(solution)/shard_map/ppermute | solution.py:374
  27.2 17.1 %collective-permute-start.2 = (bf16[512,256]{1,0:T(8,128)(2,1)S(1)}, bf16[512,256]{1,0:T(8,128)(2,1)S(1)}, u32[]{:S(2)}, u32[]{:S(2)}) collective-permute-start(bf16[512,256]{1,0:T(8,128)(2,1)S(1)} %get-tuple-element.26), channel_id=1, source_target_pairs={{0,64},{32,96},{64,0},{96,32},{1,65},{33,97},{65,1},{97,33},{2,66}... | collective-permute-start | bytes 786440 | tf_op jit(solution)/shard_map/ppermute | solution.py:374
  48.4 19.3 %copy-start.6 = (s32[5]{0:T(128)S(1)}, s32[5]{0:T(128)}, u32[]{:S(2)}) copy-start(s32[5]{0:T(128)} %constant.127.clone) | copy-start | bytes 64
  48.4 19.3 %copy-start.7 = (s32[5]{0:T(128)S(1)}, s32[5]{0:T(128)}, u32[]{:S(2)}) copy-start(s32[5]{0:T(128)} %constant.126.clone) | copy-start | bytes 64
  48.4 14.5 %all-to-all-start.1 = ((bf16[16,8,1024]{2,1,0:T(8,128)(2,1)}), bf16[16,8,1024]{2,1,0:T(8,128)(2,1)S(1)}, u32[]{:S(2)}, u32[]{:S(2)}) async-start(bf16[16,8,1024]{2,1,0:T(8,128)(2,1)} %bitcast.4), calls=%async_computation.1 | async-start | bytes 524288 | tf_op jit(solution)/shard_map/all_to_all | solution.py:378
  52.3 38.6 %collective-permute-start.9 = (bf16[1536,256]{1,0:T(8,128)(2,1)S(1)}, bf16[1536,256]{1,0:T(8,128)(2,1)}, u32[]{:S(2)}, u32[]{:S(2)}) collective-permute-start(bf16[1536,256]{1,0:T(8,128)(2,1)S(1)} %pad_maximum_fusion.refs_0_), channel_id=1, source_target_pairs={{0,2},{2,4},{4,6},{6,0},{1,3},{3,5},{5,7},{7,1},{8,10},{10,12},{12... | collective-permute-start | bytes 2359304 | tf_op jit(solution)/shard_map/ppermute | solution.py:374
  53.6 37.3 %collective-permute-start.8 = (bf16[1536,256]{1,0:T(8,128)(2,1)S(1)}, bf16[1536,256]{1,0:T(8,128)(2,1)}, u32[]{:S(2)}, u32[]{:S(2)}) collective-permute-start(bf16[1536,256]{1,0:T(8,128)(2,1)S(1)} %pad_maximum_fusion.refs_0_), channel_id=1, source_target_pairs={{0,4},{2,6},{4,0},{6,2},{1,5},{3,7},{5,1},{7,3},{8,12},{10,14},{12... | collective-permute-start | bytes 2359304 | tf_op jit(solution)/shard_map/ppermute | solution.py:374
  56.2 34.7 %collective-permute-start.7 = (bf16[1536,256]{1,0:T(8,128)(2,1)S(1)}, bf16[1536,256]{1,0:T(8,128)(2,1)}, u32[]{:S(2)}, u32[]{:S(2)}) collective-permute-start(bf16[1536,256]{1,0:T(8,128)(2,1)S(1)} %pad_maximum_fusion.refs_0_), channel_id=1, source_target_pairs={{0,6},{2,0},{4,2},{6,4},{1,7},{3,1},{5,3},{7,5},{8,14},{10,8},{12,... | collective-permute-start | bytes 2359304 | tf_op jit(solution)/shard_map/ppermute | solution.py:374
  64.0 16.4 %all-to-all-start.2 = ((bf16[16,12,1024]{2,1,0:T(8,128)(2,1)}), bf16[16,12,1024]{2,1,0:T(8,128)(2,1)S(1)}, u32[]{:S(2)}, u32[]{:S(2)}) async-start(bf16[16,12,1024]{2,1,0:T(8,128)(2,1)} %broadcast_in_dim.20), calls=%async_computation.2 | async-start | bytes 1048576 | tf_op jit(solution)/shard_map/all_to_all | solution.py:378
  67.6 97.9 %reduce-scatter.2.cloned.1.call-start = ((), (), s32[]{:S(2)}) async-start(), calls=%async_computation.7 | async-start | bytes 5242880 | tf_op jit(solution)/shard_map/reduce_scatter | solution.py:485
  71.5 19.4 %collective-permute-start.6 = (bf16[256,1024]{1,0:T(8,128)(2,1)}, bf16[256,1024]{1,0:T(8,128)(2,1)}, u32[]{:S(2)}, u32[]{:S(2)}) collective-permute-start(bf16[256,1024]{1,0:T(8,128)(2,1)} %slice.36), channel_id=1, source_target_pairs={{0,24},{8,0},{16,8},{24,16},{1,25},{9,1},{17,9},{25,17},{2,26},{10... | collective-permute-start | bytes 1572872 | tf_op jit(solution)/shard_map/ppermute | solution.py:374
  74.0 17.0 %collective-permute-start.5 = (bf16[256,1024]{1,0:T(8,128)(2,1)}, bf16[256,1024]{1,0:T(8,128)(2,1)}, u32[]{:S(2)}, u32[]{:S(2)}) collective-permute-start(bf16[256,1024]{1,0:T(8,128)(2,1)} %slice.35), channel_id=1, source_target_pairs={{0,8},{8,16},{16,24},{24,0},{1,9},{9,17},{17,25},{25,1},{2,10},{10... | collective-permute-start | bytes 1572872 | tf_op jit(solution)/shard_map/ppermute | solution.py:374
  80.5 1.2 copy-start.2
  81.7 1.2 copy-start.3
  90.9 5.8 %collective-permute-start.10 = (bf16[1536,256]{1,0:T(8,128)(2,1)S(1)}, bf16[1536,256]{1,0:T(8,128)(2,1)S(1)}, u32[]{:S(2)}, u32[]{:S(2)}) collective-permute-start(bf16[1536,256]{1,0:T(8,128)(2,1)S(1)} %pad_maximum_fusion.refs_0_), channel_id=1, source_target_pairs={{0,1},{1,0},{2,3},{3,2},{4,5},{5,4},{6,7},{7,6},{8,9},{9,8},{10,11... | collective-permute-start | bytes 2359304 | tf_op jit(solution)/shard_map/ppermute | solution.py:374
  94.6 3.2 %collective-permute-start.11 = (bf16[1536,256]{1,0:T(8,128)(2,1)}, bf16[1536,256]{1,0:T(8,128)(2,1)S(1)}, u32[]{:S(2)}, u32[]{:S(2)}) collective-permute-start(bf16[1536,256]{1,0:T(8,128)(2,1)} %collective-permute-done.7.refs_1_), channel_id=1, source_target_pairs={{0,1},{1,0},{2,3},{3,2},{4,5},{5,4},{6,7},{7,6},{8,9},{9,8},{10,11... | collective-permute-start | bytes 2359304 | tf_op jit(solution)/shard_map/ppermute | solution.py:374
  94.7 4.3 %collective-permute-start.12 = (bf16[1536,256]{1,0:T(8,128)(2,1)}, bf16[1536,256]{1,0:T(8,128)(2,1)S(1)}, u32[]{:S(2)}, u32[]{:S(2)}) collective-permute-start(bf16[1536,256]{1,0:T(8,128)(2,1)} %collective-permute-done.8.refs_2_), channel_id=1, source_target_pairs={{0,1},{1,0},{2,3},{3,2},{4,5},{5,4},{6,7},{7,6},{8,9},{9,8},{10,11... | collective-permute-start | bytes 2359304 | tf_op jit(solution)/shard_map/ppermute | solution.py:374
  95.2 5.0 %collective-permute-start.13 = (bf16[1536,256]{1,0:T(8,128)(2,1)}, bf16[1536,256]{1,0:T(8,128)(2,1)S(1)}, u32[]{:S(2)}, u32[]{:S(2)}) collective-permute-start(bf16[1536,256]{1,0:T(8,128)(2,1)} %collective-permute-done.9.refs_3_), channel_id=1, source_target_pairs={{0,1},{1,0},{2,3},{3,2},{4,5},{5,4},{6,7},{7,6},{8,9},{9,8},{10,11... | collective-permute-start | bytes 2359304 | tf_op jit(solution)/shard_map/ppermute | solution.py:374
  99.0 1.1 copy-start.8
  100.1 0.9 copy-start.9
  115.0 0.7 copy-start.12
  117.0 2.2 %copy-start.1 = (bf16[8192,256]{1,0:T(8,128)(2,1)S(1)}, bf16[8192,256]{1,0:T(8,128)(2,1)}, u32[]{:S(2)}) copy-start(bf16[8192,256]{1,0:T(8,128)(2,1)} %all-gather.2.cloned.1.call-done.w_ref) | copy-start | bytes 12582916
  152.4 12.5 %all-to-all-start.5 = ((f32[8,16,512]{2,1,0:T(8,128)}), f32[8,16,512]{2,1,0:T(8,128)S(1)}, u32[]{:S(2)}, u32[]{:S(2)}) async-start(f32[8,16,512]{2,1,0:T(8,128)} %fusion), calls=%async_computation.6 | async-start | bytes 524288 | tf_op jit(solution)/shard_map/all_to_all | solution.py:378
  165.6 1.2 copy-start.4
Sparse Core Ops, SparseCore 0:
  11.2 64.9 all-gather.1
Sparse Core Ops, SparseCore 1:
  115.1 50.4 reduce-scatter.1

commit v4 on v3

--- a/solution.py
+++ b/solution.py
@@ -136,13 +136,17 @@
         if b > 0:
             for copy in copies[(b - 1) * count : b * count]:
                 copy.wait()
-        for n in range(0, w_v.shape[1], COLS):
+        for i, n in enumerate(range(0, w_v.shape[1], COLS)):
             o_v[b, :, n : n + COLS] = jnp.dot(
                 t_v[b], w_v[:, n : n + COLS], preferred_element_type=F32
             ).astype(BF16)
-        copy = pltpu.make_async_copy(o_v.at[b], out_ref.at[place_ref[b]], o_sem.at[b])
-        copy.start()
-        out_copies.append(copy)
+            copy = pltpu.make_async_copy(
+                o_v.at[b, :, pl.ds(n, COLS)],
+                out_ref.at[place_ref[b], :, pl.ds(n, COLS)],
+                o_sem.at[b, i],
+            )
+            copy.start()
+            out_copies.append(copy)
     for copy in out_copies:
         copy.wait()
 
@@ -167,7 +171,7 @@
                 pltpu.SemaphoreType.DMA((blocks - 1, len(pieces))),
                 pltpu.SemaphoreType.DMA,
                 pltpu.SemaphoreType.DMA((len(weights),)),
-                pltpu.SemaphoreType.DMA((blocks,)),
+                pltpu.SemaphoreType.DMA((blocks, cols // COLS)),
             ],
         ),
         out_shape=jax.ShapeDtypeStruct((blocks, rows, cols), BF16),
@@ -477,9 +481,9 @@
     context = exchange(combine(sums), HST)
     product = jnp.dot(
         context.reshape(N_HST * query_rows, query_cols), w_output, preferred_element_type=F32
-    )
+    ).astype(BF16)
     product = exchange(product.reshape(N_HEAD, -1, product.shape[1]), HEAD)
-    query_output = jnp.sum(product, axis=0).astype(BF16)
+    query_output = jnp.sum(product.astype(F32), axis=0).astype(BF16)
 
     products = share_products(spots, fresh_states, pieces, weights)
     queries = lax.psum_scatter(

time: 182 us -> 182 us (level)
  blocking collectives: 23.7 us -> 11.8 us
  waiting for transfers between devices: 41.7 us -> 48.4 us
  starting transfers between devices: 39.4 us -> 43.9 us
    all_to_all x2 -> x1, blocking collectives: 23.7 us -> 11.8 us  [exchange(): return lax.all_to_all(value, axis, 0, 0, tiled=True)]
    all_to_all x4 -> x5, waiting for transfers between devices: 21.3 us -> 27.6 us  [exchange(): return lax.all_to_all(value, axis, 0, 0, tiled=True)]
    all_to_all x4 -> x5, starting transfers between devices: 19.7 us -> 24.1 us  [exchange(): return lax.all_to_all(value, axis, 0, 0, tiled=True)]
  transfers between devices with their start and end apart: 20 -> 21, of which waited for: 10 -> 12; matrix products, arithmetic and copies ran while one was open for 7% -> 7% of each run, Pallas kernels for 17% -> 17%
where the time goes in v4:
time: 182 us; the launch traced here: 181 us
  waiting for transfers between devices  48.4 us (27%)
  starting transfers between devices  43.9 us (24%)
  Pallas kernels  37.6 us (21%)
  between operations  16.5 us (9%)
  local copies, waits for them, and re-layouts  13.7 us (8%)
  blocking collectives  11.8 us (6%)
  other arithmetic  6.8 us (4%)
  matrix products  1.98 us (1%)
    all_to_all x5, waiting for transfers between devices, exchange(): return lax.all_to_all(value, axis, 0, 0, tiled=True)  27.6 us
    all_to_all x5, starting transfers between devices, exchange(): return lax.all_to_all(value, axis, 0, 0, tiled=True)  24.1 us
    ppermute x14, waiting for transfers between devices, shift(): lax.ppermute(value, axis, [(i, (i + by) % size) for i in range(size)])  20.3 us
    ppermute x14, starting transfers between devices, shift(): lax.ppermute(value, axis, [(i, (i + by) % size) for i in range(size)])  19.7 us
    pallas_call x1, Pallas kernels, share_products(): pl.pallas_call(functools.partial(shares_kernel, len(pieces)), grid_spec=p...  13.8 us
    all_to_all x1, blocking collectives, exchange(): return lax.all_to_all(value, axis, 0, 0, tiled=True)  11.8 us
    pallas_call x1, Pallas kernels, cached_attention(): pl.pallas_call(cached_kernel, grid=(cols // wide,), in_specs=[pl.BlockSpe...  7.94 us
    unnamed x29, local copies, waits for them, and re-layouts  7.51 us
  transfers between devices with their start and end apart: 21, of which 12 were waited for; matrix products, arithmetic and copies ran while one was open for 7% of the time, Pallas kernels for 17%

profile of v4, /device:TPU:1, one launch (start us, length us, event | category | flops | bytes accessed | tf_op | source)
XLA Modules:
  0.0 180.7 jit_solution(16918089349497725380)
XLA Ops:
  8.1 1.8 pad_maximum_fusion.4
  9.9 2.1 %collective-permute-start.3 = (bf16[512,1024]{1,0:T(8,128)(2,1)}, bf16[512,1024]{1,0:T(8,128)(2,1)}, u32[]{:S(2)}, u32[]{:S(2)}) collective-permute-start(bf16[512,1024]{1,0:T(8,128)(2,1)} %refs_8_.1), channel_id=1, source_target_pairs={{0,8},{8,16},{16,24},{24,0},{1,9},{9,17},{17,25},{25,1},{2,10},{10... | collective-permute-start | bytes 3145736 | tf_op jit(solution)/shard_map/ppermute | solution.py:378
  12.0 1.4 collective-permute-start.4
  14.1 0.9 dynamic-slice_select_fusion
  15.0 1.7 pad_maximum_fusion.1
  16.7 1.3 constant_dynamic-slice_fusion
  18.0 6.5 %all-to-all-start = ((bf16[16,16,512]{2,1,0:T(8,128)(2,1)}), bf16[16,16,512]{2,1,0:T(8,128)(2,1)S(1)}, u32[]{:S(2)}, u32[]{:S(2)}) async-start(bf16[16,16,512]{2,1,0:T(8,128)(2,1)} %pad_maximum_fusion.1), calls=%async_computation | async-start | bytes 524288 | tf_op jit(solution)/shard_map/all_to_all | solution.py:382
  24.5 1.4 collective-permute-start
  25.9 1.4 collective-permute-start.1
  27.3 1.6 collective-permute-start.2
  29.0 8.2 %collective-permute-done = bf16[512,256]{1,0:T(8,128)(2,1)S(1)} collective-permute-done((bf16[512,256]{1,0:T(8,128)(2,1)S(1)}, bf16[512,256]{1,0:T(8,128)(2,1)S(1)}, u32[]{:S(2)}, u32[]{:S(2)}) %collective-permute-start) | collective-permute-done | bytes 262176 | tf_op jit(solution)/shard_map/ppermute | solution.py:378
  37.2 7.2 %collective-permute-done.2 = bf16[512,256]{1,0:T(8,128)(2,1)S(1)} collective-permute-done((bf16[512,256]{1,0:T(8,128)(2,1)S(1)}, bf16[512,256]{1,0:T(8,128)(2,1)S(1)}, u32[]{:S(2)}, u32[]{:S(2)}) %collective-permute-start.2) | collective-permute-done | bytes 262176 | tf_op jit(solution)/shard_map/ppermute | solution.py:378
  44.4 3.0 %all-to-all-done = bf16[16,16,512]{2,1,0:T(8,128)(2,1)S(1)} async-done(((bf16[16,16,512]{2,1,0:T(8,128)(2,1)}), bf16[16,16,512]{2,1,0:T(8,128)(2,1)S(1)}, u32[]{:S(2)}, u32[]{:S(2)}) %all-to-all-start) | async-done | bytes 262176 | tf_op jit(solution)/shard_map/all_to_all | solution.py:382
  47.4 1.0 convolution_convert_fusion
  48.4 3.7 %all-to-all-start.1 = ((bf16[16,8,1024]{2,1,0:T(8,128)(2,1)}), bf16[16,8,1024]{2,1,0:T(8,128)(2,1)S(1)}, u32[]{:S(2)}, u32[]{:S(2)}) async-start(bf16[16,8,1024]{2,1,0:T(8,128)(2,1)} %bitcast.4), calls=%async_computation.1 | async-start | bytes 524288 | tf_op jit(solution)/shard_map/all_to_all | solution.py:382
  52.3 1.3 collective-permute-start.9
  53.6 2.6 %collective-permute-start.8 = (bf16[1536,256]{1,0:T(8,128)(2,1)S(1)}, bf16[1536,256]{1,0:T(8,128)(2,1)}, u32[]{:S(2)}, u32[]{:S(2)}) collective-permute-start(bf16[1536,256]{1,0:T(8,128)(2,1)S(1)} %pad_maximum_fusion.refs_0_), channel_id=1, source_target_pairs={{0,4},{2,6},{4,0},{6,2},{1,5},{3,7},{5,1},{7,3},{8,12},{10,14},{12... | collective-permute-start | bytes 2359304 | tf_op jit(solution)/shard_map/ppermute | solution.py:378
  56.3 1.1 collective-permute-start.7
  57.4 5.6 %all-to-all-done.1 = bf16[16,8,1024]{2,1,0:T(8,128)(2,1)S(1)} async-done(((bf16[16,8,1024]{2,1,0:T(8,128)(2,1)}), bf16[16,8,1024]{2,1,0:T(8,128)(2,1)S(1)}, u32[]{:S(2)}, u32[]{:S(2)}) %all-to-all-start.1) | async-done | bytes 262176 | tf_op jit(solution)/shard_map/all_to_all | solution.py:382
  63.2 0.8 broadcast_in_dim.20
  64.1 3.6 %all-to-all-start.2 = ((bf16[16,12,1024]{2,1,0:T(8,128)(2,1)}), bf16[16,12,1024]{2,1,0:T(8,128)(2,1)S(1)}, u32[]{:S(2)}, u32[]{:S(2)}) async-start(bf16[16,12,1024]{2,1,0:T(8,128)(2,1)} %broadcast_in_dim.20), calls=%async_computation.2 | async-start | bytes 1048576 | tf_op jit(solution)/shard_map/all_to_all | solution.py:382
  67.8 1.9 %slice.35 = bf16[256,1024]{1,0:T(8,128)(2,1)} slice(bf16[512,1024]{1,0:T(8,128)(2,1)} %collective-permute-done.3.refs_10_), slice={[0:256], [0:1024]} | slice | bytes 1048576 | tf_op jit(solution)/shard_map/slice | solution.py:455
  69.7 1.9 %slice.36 = bf16[256,1024]{1,0:T(8,128)(2,1)} slice(bf16[512,1024]{1,0:T(8,128)(2,1)} %collective-permute-done.4.refs_9_), slice={[256:512], [0:1024]} | slice | bytes 1048576 | tf_op jit(solution)/shard_map/slice | solution.py:455
  71.5 2.5 %collective-permute-start.6 = (bf16[256,1024]{1,0:T(8,128)(2,1)}, bf16[256,1024]{1,0:T(8,128)(2,1)}, u32[]{:S(2)}, u32[]{:S(2)}) collective-permute-start(bf16[256,1024]{1,0:T(8,128)(2,1)} %slice.36), channel_id=1, source_target_pairs={{0,24},{8,0},{16,8},{24,16},{1,25},{9,1},{17,9},{25,17},{2,26},{10... | collective-permute-start | bytes 1572872 | tf_op jit(solution)/shard_map/ppermute | solution.py:378
  74.2 6.2 %all-to-all-done.2 = bf16[16,12,1024]{2,1,0:T(8,128)(2,1)S(1)} async-done(((bf16[16,12,1024]{2,1,0:T(8,128)(2,1)}), bf16[16,12,1024]{2,1,0:T(8,128)(2,1)S(1)}, u32[]{:S(2)}, u32[]{:S(2)}) %all-to-all-start.2) | async-done | bytes 393248 | tf_op jit(solution)/shard_map/all_to_all | solution.py:382
  80.4 1.2 copy-done.2
  81.6 1.2 copy-done.3
  82.9 7.9 %cached_attention.1 = (f32[128,1024]{1,0:T(8,128)S(1)}, f32[128,128]{1,0:T(8,128)S(1)}) custom-call(bf16[128,1024]{1,0:T(8,128)(2,1)S(1)} %slice_bitcast_fusion.q_ref, bf16[4096,128]{1,0:T(8,128)(2,1)S(1)} %bitcast.57, bf16[4096,128]{1,0:T(8,128)(2,1)S(1)} %bitcast.56, f32[1,4096]{1,0:T(1,128)S(1)} %bitcast.55), custom_call_target="tpu_custom_call" | custom-call | flops 2147483648 | bytes 2621440 | tf_op jit(solution)/shard_map/cached_attention/pallas_call | solution.py:284
  90.9 3.8 %collective-permute-start.10 = (bf16[1536,256]{1,0:T(8,128)(2,1)S(1)}, bf16[1536,256]{1,0:T(8,128)(2,1)S(1)}, u32[]{:S(2)}, u32[]{:S(2)}) collective-permute-start(bf16[1536,256]{1,0:T(8,128)(2,1)S(1)} %pad_maximum_fusion.refs_0_), channel_id=1, source_target_pairs={{0,1},{1,0},{2,3},{3,2},{4,5},{5,4},{6,7},{7,6},{8,9},{9,8},{10,11... | collective-permute-start | bytes 2359304 | tf_op jit(solution)/shard_map/ppermute | solution.py:378
  95.3 1.5 collective-permute-done.10.refs_4_
  96.8 1.1 collective-permute-done.11.refs_5_
  97.9 1.1 collective-permute-done.12.refs_6_
  99.0 1.1 collective-permute-done.13.refs_7_
  100.2 0.9 copy-done.9
  101.1 13.8 %share_products.1 = bf16[4,512,1024]{2,1,0:T(8,128)(2,1)} custom-call(s32[17]{0:T(128)S(1)} %concatenate.40.place_ref, bf16[512,8192]{1,0:T(8,128)(2,1)} %states_ref.3, bf16[1536,256]{1,0:T(8,128)(2,1)S(1)} %pad_maximum_fusion.refs_0_, bf16[1536,256]{1,0:T(8,128)(2,1)} %collective-permute-done.7.refs_1_, bf16[1536,256]{1,0:T(8,128)(2,1)} %collective-permute-done.8.refs_2_, ...), custom_call_target="tpu_custom_call" | custom-call | flops 8589934592 | bytes 16777216 | tf_op jit(solution)/shard_map/share_products/pallas_call | solution.py:160
  115.6 1.0 fusion.3
  116.9 2.2 %copy-done.1 = bf16[8192,256]{1,0:T(8,128)(2,1)S(1)} copy-done((bf16[8192,256]{1,0:T(8,128)(2,1)S(1)}, bf16[8192,256]{1,0:T(8,128)(2,1)}, u32[]{:S(2)}) %copy-start.1) | copy-done | bytes 4194328
  119.1 5.9 %key_value.1 = (bf16[512,128]{1,0:T(8,128)(2,1)S(1)}, bf16[512,128]{1,0:T(8,128)(2,1)S(1)}) custom-call(bf16[512,8192]{1,0:T(8,128)(2,1)} %states_ref.3, bf16[8192,256]{1,0:T(8,128)(2,1)S(1)} %copy-done.1, f32[512,128]{1,0:T(8,128)S(1)} %get-tuple-element.63.cos_ref.refs_1_, f32[512,128]{1,0:T(8,128)S(1)} %get-tuple-element.64.sin_ref.refs_2_), custom_call_target="tpu_custom_call" | custom-call | flops 2147483648 | bytes 12582912 | tf_op jit(solution)/shard_map/key_value/pallas_call | solution.py:210
  125.0 2.3 %context_attention.1 = bf16[128,1152]{1,0:T(8,128)(2,1)S(1)} custom-call(bf16[128,1024]{1,0:T(8,128)(2,1)S(1)} %slice_bitcast_fusion.q_ref, bf16[512,128]{1,0:T(8,128)(2,1)S(1)} %get-tuple-element.40.refs_3_.k_ref, bf16[512,128]{1,0:T(8,128)(2,1)S(1)} %get-tuple-element.41.refs_4_.v_ref, f32[128,1024]{1,0:T(8,128)S(1)} %get-tuple-element.42.old_ref, ...), custom_call_target="tpu_custom_call" | custom-call | flops 268435456 | bytes 1310720 | tf_op jit(solution)/shard_map/context_attention/pallas_call | solution.py:334
  127.2 11.8 %all_to_all.30.parts_ref = bf16[16,8,1152]{2,1,0:T(8,128)(2,1)S(1)} all-to-all(bf16[16,8,1152]{2,1,0:T(8,128)(2,1)S(1)} %bitcast.52), channel_id=1, replica_groups=mesh['z'=4,'x'=4,'y'=4,'core'=2] {'z','x'}, dimensions={0} | all-to-all | bytes 589824 | tf_op jit(solution)/shard_map/all_to_all | solution.py:382
  139.1 1.1 combine.1
  140.2 4.4 %all-to-all-start.4 = ((bf16[16,8,1024]{2,1,0:T(8,128)(2,1)}), bf16[16,8,1024]{2,1,0:T(8,128)(2,1)S(1)}, u32[]{:S(2)}, u32[]{:S(2)}) async-start(bf16[16,8,1024]{2,1,0:T(8,128)(2,1)} %combine.1), calls=%async_computation.5 | async-start | bytes 524288 | tf_op jit(solution)/shard_map/all_to_all | solution.py:382
  144.7 7.5 %all-to-all-done.4 = bf16[16,8,1024]{2,1,0:T(8,128)(2,1)S(1)} async-done(((bf16[16,8,1024]{2,1,0:T(8,128)(2,1)}), bf16[16,8,1024]{2,1,0:T(8,128)(2,1)S(1)}, u32[]{:S(2)}, u32[]{:S(2)}) %all-to-all-start.4) | async-done | bytes 262176 | tf_op jit(solution)/shard_map/all_to_all | solution.py:382
  152.2 1.0 convolution_convert_fusion.1
  153.2 6.0 %all-to-all-start.5 = ((bf16[8,16,512]{2,1,0:T(8,128)(2,1)}), bf16[8,16,512]{2,1,0:T(8,128)(2,1)S(1)}, u32[]{:S(2)}, u32[]{:S(2)}) async-start(bf16[8,16,512]{2,1,0:T(8,128)(2,1)} %bitcast.20), calls=%async_computation.6 | async-start | bytes 262144 | tf_op jit(solution)/shard_map/all_to_all | solution.py:382
  159.2 5.3 %all-to-all-done.5 = bf16[8,16,512]{2,1,0:T(8,128)(2,1)S(1)} async-done(((bf16[8,16,512]{2,1,0:T(8,128)(2,1)}), bf16[8,16,512]{2,1,0:T(8,128)(2,1)S(1)}, u32[]{:S(2)}, u32[]{:S(2)}) %all-to-all-start.5) | async-done | bytes 131104 | tf_op jit(solution)/shard_map/all_to_all | solution.py:382
  165.5 1.2 copy-done.4
  166.7 6.5 %fresh_attention.1 = bf16[512,1024]{1,0:T(8,128)(2,1)} custom-call(bf16[512,1024]{1,0:T(8,128)(2,1)S(1)} %copy-done.4, f32[512,128]{1,0:T(8,128)S(1)} %get-tuple-element.63.cos_ref.refs_1_, f32[512,128]{1,0:T(8,128)S(1)} %get-tuple-element.64.sin_ref.refs_2_, bf16[512,128]{1,0:T(8,128)(2,1)S(1)} %get-tuple-element.40.refs_3_.k_ref, ...), custom_call_target="tpu_custom_call" | custom-call | flops 1073741824 | bytes 2097152 | tf_op jit(solution)/shard_map/fresh_attention/pallas_call | solution.py:87
  (68 shorter events, 3.7 us)
Async XLA Ops:
  8.0 144.2 %copy-start = (bf16[1024,512]{1,0:T(8,128)(2,1)S(1)}, bf16[1024,512]{1,0:T(8,128)(2,1)}, u32[]{:S(2)}) copy-start(bf16[1024,512]{1,0:T(8,128)(2,1)} %param.19) | copy-start | bytes 3145732
  8.0 108.8 %all-gather.2.cloned.1.call-start = ((), (), s32[]{:S(2)}) async-start(), calls=%async_computation.8 | async-start | bytes 4456448 | tf_op jit(solution)/shard_map/all_gather | solution.py:408
  9.9 38.6 %collective-permute-start.3 = (bf16[512,1024]{1,0:T(8,128)(2,1)}, bf16[512,1024]{1,0:T(8,128)(2,1)}, u32[]{:S(2)}, u32[]{:S(2)}) collective-permute-start(bf16[512,1024]{1,0:T(8,128)(2,1)} %refs_8_.1), channel_id=1, source_target_pairs={{0,8},{8,16},{16,24},{24,0},{1,9},{9,17},{17,25},{25,1},{2,10},{10... | collective-permute-start | bytes 3145736 | tf_op jit(solution)/shard_map/ppermute | solution.py:378
  12.0 36.5 %collective-permute-start.4 = (bf16[512,1024]{1,0:T(8,128)(2,1)}, bf16[512,1024]{1,0:T(8,128)(2,1)}, u32[]{:S(2)}, u32[]{:S(2)}) collective-permute-start(bf16[512,1024]{1,0:T(8,128)(2,1)} %refs_8_.1), channel_id=1, source_target_pairs={{0,24},{8,0},{16,8},{24,16},{1,25},{9,1},{17,9},{25,17},{2,26},{10... | collective-permute-start | bytes 3145736 | tf_op jit(solution)/shard_map/ppermute | solution.py:378
  14.0 14.8 %copy-start.10 = (s32[16]{0:T(128)S(1)}, s32[16]{0:T(128)}, u32[]{:S(2)}) copy-start(s32[16]{0:T(128)} %param.22) | copy-start | bytes 196
  14.0 14.8 %copy-start.11 = (s32[8]{0:T(128)S(1)}, s32[8]{0:T(128)}, u32[]{:S(2)}) copy-start(s32[8]{0:T(128)} %param.25) | copy-start | bytes 100
  16.7 30.7 %copy-start.5 = (bf16[512,1024]{1,0:T(8,128)(2,1)S(1)}, bf16[512,1024]{1,0:T(8,128)(2,1)}, u32[]{:S(2)}) copy-start(bf16[512,1024]{1,0:T(8,128)(2,1)} %refs_8_.1) | copy-start | bytes 3145732
  18.0 29.4 %all-to-all-start = ((bf16[16,16,512]{2,1,0:T(8,128)(2,1)}), bf16[16,16,512]{2,1,0:T(8,128)(2,1)S(1)}, u32[]{:S(2)}, u32[]{:S(2)}) async-start(bf16[16,16,512]{2,1,0:T(8,128)(2,1)} %pad_maximum_fusion.1), calls=%async_computation | async-start | bytes 524288 | tf_op jit(solution)/shard_map/all_to_all | solution.py:382
  24.5 12.7 %collective-permute-start = (bf16[512,256]{1,0:T(8,128)(2,1)S(1)}, bf16[512,256]{1,0:T(8,128)(2,1)S(1)}, u32[]{:S(2)}, u32[]{:S(2)}) collective-permute-start(bf16[512,256]{1,0:T(8,128)(2,1)S(1)} %get-tuple-element.24), channel_id=1, source_target_pairs={{0,32},{32,64},{64,96},{96,0},{1,33},{33,65},{65,97},{97,1},{2,34}... | collective-permute-start | bytes 786440 | tf_op jit(solution)/shard_map/ppermute | solution.py:378
  25.9 11.3 %collective-permute-start.1 = (bf16[512,256]{1,0:T(8,128)(2,1)S(1)}, bf16[512,256]{1,0:T(8,128)(2,1)S(1)}, u32[]{:S(2)}, u32[]{:S(2)}) collective-permute-start(bf16[512,256]{1,0:T(8,128)(2,1)S(1)} %get-tuple-element.25), channel_id=1, source_target_pairs={{0,96},{32,0},{64,32},{96,64},{1,97},{33,1},{65,33},{97,65},{2,98}... | collective-permute-start | bytes 786440 | tf_op jit(solution)/shard_map/ppermute | solution.py:378
  27.3 17.1 %collective-permute-start.2 = (bf16[512,256]{1,0:T(8,128)(2,1)S(1)}, bf16[512,256]{1,0:T(8,128)(2,1)S(1)}, u32[]{:S(2)}, u32[]{:S(2)}) collective-permute-start(bf16[512,256]{1,0:T(8,128)(2,1)S(1)} %get-tuple-element.26), channel_id=1, source_target_pairs={{0,64},{32,96},{64,0},{96,32},{1,65},{33,97},{65,1},{97,33},{2,66}... | collective-permute-start | bytes 786440 | tf_op jit(solution)/shard_map/ppermute | solution.py:378
  48.4 19.3 %copy-start.6 = (s32[5]{0:T(128)S(1)}, s32[5]{0:T(128)}, u32[]{:S(2)}) copy-start(s32[5]{0:T(128)} %constant.128.clone) | copy-start | bytes 64
  48.4 19.3 %copy-start.7 = (s32[5]{0:T(128)S(1)}, s32[5]{0:T(128)}, u32[]{:S(2)}) copy-start(s32[5]{0:T(128)} %constant.127.clone) | copy-start | bytes 64
  48.4 14.6 %all-to-all-start.1 = ((bf16[16,8,1024]{2,1,0:T(8,128)(2,1)}), bf16[16,8,1024]{2,1,0:T(8,128)(2,1)S(1)}, u32[]{:S(2)}, u32[]{:S(2)}) async-start(bf16[16,8,1024]{2,1,0:T(8,128)(2,1)} %bitcast.4), calls=%async_computation.1 | async-start | bytes 524288 | tf_op jit(solution)/shard_map/all_to_all | solution.py:382
  52.3 38.5 %collective-permute-start.9 = (bf16[1536,256]{1,0:T(8,128)(2,1)S(1)}, bf16[1536,256]{1,0:T(8,128)(2,1)}, u32[]{:S(2)}, u32[]{:S(2)}) collective-permute-start(bf16[1536,256]{1,0:T(8,128)(2,1)S(1)} %pad_maximum_fusion.refs_0_), channel_id=1, source_target_pairs={{0,2},{2,4},{4,6},{6,0},{1,3},{3,5},{5,7},{7,1},{8,10},{10,12},{12... | collective-permute-start | bytes 2359304 | tf_op jit(solution)/shard_map/ppermute | solution.py:378
  53.6 37.2 %collective-permute-start.8 = (bf16[1536,256]{1,0:T(8,128)(2,1)S(1)}, bf16[1536,256]{1,0:T(8,128)(2,1)}, u32[]{:S(2)}, u32[]{:S(2)}) collective-permute-start(bf16[1536,256]{1,0:T(8,128)(2,1)S(1)} %pad_maximum_fusion.refs_0_), channel_id=1, source_target_pairs={{0,4},{2,6},{4,0},{6,2},{1,5},{3,7},{5,1},{7,3},{8,12},{10,14},{12... | collective-permute-start | bytes 2359304 | tf_op jit(solution)/shard_map/ppermute | solution.py:378
  56.3 34.6 %collective-permute-start.7 = (bf16[1536,256]{1,0:T(8,128)(2,1)S(1)}, bf16[1536,256]{1,0:T(8,128)(2,1)}, u32[]{:S(2)}, u32[]{:S(2)}) collective-permute-start(bf16[1536,256]{1,0:T(8,128)(2,1)S(1)} %pad_maximum_fusion.refs_0_), channel_id=1, source_target_pairs={{0,6},{2,0},{4,2},{6,4},{1,7},{3,1},{5,3},{7,5},{8,14},{10,8},{12,... | collective-permute-start | bytes 2359304 | tf_op jit(solution)/shard_map/ppermute | solution.py:378
  64.1 16.3 %all-to-all-start.2 = ((bf16[16,12,1024]{2,1,0:T(8,128)(2,1)}), bf16[16,12,1024]{2,1,0:T(8,128)(2,1)S(1)}, u32[]{:S(2)}, u32[]{:S(2)}) async-start(bf16[16,12,1024]{2,1,0:T(8,128)(2,1)} %broadcast_in_dim.20), calls=%async_computation.2 | async-start | bytes 1048576 | tf_op jit(solution)/shard_map/all_to_all | solution.py:382
  67.6 97.8 %reduce-scatter.2.cloned.1.call-start = ((), (), s32[]{:S(2)}) async-start(), calls=%async_computation.7 | async-start | bytes 5242880 | tf_op jit(solution)/shard_map/reduce_scatter | solution.py:489
  71.5 19.3 %collective-permute-start.6 = (bf16[256,1024]{1,0:T(8,128)(2,1)}, bf16[256,1024]{1,0:T(8,128)(2,1)}, u32[]{:S(2)}, u32[]{:S(2)}) collective-permute-start(bf16[256,1024]{1,0:T(8,128)(2,1)} %slice.36), channel_id=1, source_target_pairs={{0,24},{8,0},{16,8},{24,16},{1,25},{9,1},{17,9},{25,17},{2,26},{10... | collective-permute-start | bytes 1572872 | tf_op jit(solution)/shard_map/ppermute | solution.py:378
  74.0 16.8 %collective-permute-start.5 = (bf16[256,1024]{1,0:T(8,128)(2,1)}, bf16[256,1024]{1,0:T(8,128)(2,1)}, u32[]{:S(2)}, u32[]{:S(2)}) collective-permute-start(bf16[256,1024]{1,0:T(8,128)(2,1)} %slice.35), channel_id=1, source_target_pairs={{0,8},{8,16},{16,24},{24,0},{1,9},{9,17},{17,25},{25,1},{2,10},{10... | collective-permute-start | bytes 1572872 | tf_op jit(solution)/shard_map/ppermute | solution.py:378
  80.4 1.2 copy-start.2
  81.6 1.2 copy-start.3
  90.9 5.9 %collective-permute-start.10 = (bf16[1536,256]{1,0:T(8,128)(2,1)S(1)}, bf16[1536,256]{1,0:T(8,128)(2,1)S(1)}, u32[]{:S(2)}, u32[]{:S(2)}) collective-permute-start(bf16[1536,256]{1,0:T(8,128)(2,1)S(1)} %pad_maximum_fusion.refs_0_), channel_id=1, source_target_pairs={{0,1},{1,0},{2,3},{3,2},{4,5},{5,4},{6,7},{7,6},{8,9},{9,8},{10,11... | collective-permute-start | bytes 2359304 | tf_op jit(solution)/shard_map/ppermute | solution.py:378
  94.7 3.2 %collective-permute-start.11 = (bf16[1536,256]{1,0:T(8,128)(2,1)}, bf16[1536,256]{1,0:T(8,128)(2,1)S(1)}, u32[]{:S(2)}, u32[]{:S(2)}) collective-permute-start(bf16[1536,256]{1,0:T(8,128)(2,1)} %collective-permute-done.7.refs_1_), channel_id=1, source_target_pairs={{0,1},{1,0},{2,3},{3,2},{4,5},{5,4},{6,7},{7,6},{8,9},{9,8},{10,11... | collective-permute-start | bytes 2359304 | tf_op jit(solution)/shard_map/ppermute | solution.py:378
  94.8 4.3 %collective-permute-start.12 = (bf16[1536,256]{1,0:T(8,128)(2,1)}, bf16[1536,256]{1,0:T(8,128)(2,1)S(1)}, u32[]{:S(2)}, u32[]{:S(2)}) collective-permute-start(bf16[1536,256]{1,0:T(8,128)(2,1)} %collective-permute-done.8.refs_2_), channel_id=1, source_target_pairs={{0,1},{1,0},{2,3},{3,2},{4,5},{5,4},{6,7},{7,6},{8,9},{9,8},{10,11... | collective-permute-start | bytes 2359304 | tf_op jit(solution)/shard_map/ppermute | solution.py:378
  95.2 5.0 %collective-permute-start.13 = (bf16[1536,256]{1,0:T(8,128)(2,1)}, bf16[1536,256]{1,0:T(8,128)(2,1)S(1)}, u32[]{:S(2)}, u32[]{:S(2)}) collective-permute-start(bf16[1536,256]{1,0:T(8,128)(2,1)} %collective-permute-done.9.refs_3_), channel_id=1, source_target_pairs={{0,1},{1,0},{2,3},{3,2},{4,5},{5,4},{6,7},{7,6},{8,9},{9,8},{10,11... | collective-permute-start | bytes 2359304 | tf_op jit(solution)/shard_map/ppermute | solution.py:378
  99.0 1.1 copy-start.8
  100.2 0.9 copy-start.9
  114.9 0.7 copy-start.12
  116.9 2.2 %copy-start.1 = (bf16[8192,256]{1,0:T(8,128)(2,1)S(1)}, bf16[8192,256]{1,0:T(8,128)(2,1)}, u32[]{:S(2)}) copy-start(bf16[8192,256]{1,0:T(8,128)(2,1)} %all-gather.2.cloned.1.call-done.w_ref) | copy-start | bytes 12582916
  140.2 12.0 %all-to-all-start.4 = ((bf16[16,8,1024]{2,1,0:T(8,128)(2,1)}), bf16[16,8,1024]{2,1,0:T(8,128)(2,1)S(1)}, u32[]{:S(2)}, u32[]{:S(2)}) async-start(bf16[16,8,1024]{2,1,0:T(8,128)(2,1)} %combine.1), calls=%async_computation.5 | async-start | bytes 524288 | tf_op jit(solution)/shard_map/all_to_all | solution.py:382
  153.2 11.3 %all-to-all-start.5 = ((bf16[8,16,512]{2,1,0:T(8,128)(2,1)}), bf16[8,16,512]{2,1,0:T(8,128)(2,1)S(1)}, u32[]{:S(2)}, u32[]{:S(2)}) async-start(bf16[8,16,512]{2,1,0:T(8,128)(2,1)} %bitcast.20), calls=%async_computation.6 | async-start | bytes 262144 | tf_op jit(solution)/shard_map/all_to_all | solution.py:382
  165.5 1.2 copy-start.4
Sparse Core Ops, SparseCore 0:
  11.2 64.8 all-gather.1
Sparse Core Ops, SparseCore 1:
  115.0 50.4 reduce-scatter.1
